TPU v7x, 32 devices: a whole 2x2x4 slice. The times are simulated.
32 devices in a mesh: seq: 8 (over y, x, core), fsdp: 4 (over z).
Axes of the slice: x: 2, y: 2, z: 4, core: 2. Of those that a mesh axis runs over, the one named last changes fastest.
Arguments:
- inputs: bfloat16 [8, 2048, 512], P('fsdp', 'seq'), may hold values from -6 to 6
- encoded: bfloat16 [8, 2048, 512], P('fsdp', 'seq'), may hold values from -6 to 6
- cotangent: bfloat16 [8, 2048, 512], P('fsdp', 'seq'), may hold values from -6 to 6
- seg_ids: int32 [8, 2048], P('fsdp'), may hold values from 0 to 15, never falling along the last dimension, each value on 1 to 256 neighbouring positions
- keep_mask: int32 [8, 2048], P('fsdp'), may hold values 0 or 1
- pair_tags: int32 [8, 16], P('fsdp'), may hold values from 0 to 15
- cut_lo: int32 [8, 16], P('fsdp'), may hold values from 0 to 63
- cut_hi: int32 [8, 16], P('fsdp'), may hold values from 0 to 63
- w_query: bfloat16 [512, 512], P('fsdp'), may hold values from -0.25 to 0.25
- w_key: bfloat16 [512, 512], P('fsdp'), may hold values from -0.25 to 0.25
- w_value: bfloat16 [512, 512], P('fsdp'), may hold values from -0.25 to 0.25
- w_out: bfloat16 [512, 512], P('fsdp'), may hold values from -1 to 1
- c_query: bfloat16 [512, 512], P('fsdp'), may hold values from -0.25 to 0.25
- c_key: bfloat16 [512, 512], P('fsdp'), may hold values from -0.25 to 0.25
- c_value: bfloat16 [512, 512], P('fsdp'), may hold values from -0.25 to 0.25
- c_out: bfloat16 [512, 512], P('fsdp'), may hold values from -1 to 1
- w_up: bfloat16 [512, 2048], P('fsdp'), may hold values from -0.25 to 0.25
- w_down: bfloat16 [2048, 512], P('fsdp'), may hold values from -0.25 to 0.25
- gain_one: bfloat16 [512], P('fsdp'), may hold values from 0.5 to 1.5
- bias_one: bfloat16 [512], P('fsdp'), may hold values from -3 to 3
- gain_two: bfloat16 [512], P('fsdp'), may hold values from 0.5 to 1.5
- bias_two: bfloat16 [512], P('fsdp'), may hold values from -3 to 3
- gain_three: bfloat16 [512], P('fsdp'), may hold values from 0.5 to 1.5
- bias_three: bfloat16 [512], P('fsdp'), may hold values from -3 to 3
- tag_table: bfloat16 [16, 512], P(None, 'fsdp'), may hold values from -3 to 3
Outputs:
- output: bfloat16 [8, 2048, 512], P('fsdp', 'seq')
- grad_inputs: bfloat16 [8, 2048, 512], P('fsdp', 'seq')
- grad_encoded: bfloat16 [8, 2048, 512], P('fsdp', 'seq')
- grad_w_query: float32 [512, 512], P('fsdp')
- grad_w_key: float32 [512, 512], P('fsdp')
- grad_w_value: float32 [512, 512], P('fsdp')
- grad_w_out: float32 [512, 512], P('fsdp')
- grad_c_query: float32 [512, 512], P('fsdp')
- grad_c_key: float32 [512, 512], P('fsdp')
- grad_c_value: float32 [512, 512], P('fsdp')
- grad_c_out: float32 [512, 512], P('fsdp')
- grad_w_up: float32 [512, 2048], P('fsdp')
- grad_w_down: float32 [2048, 512], P('fsdp')
- grad_gain_one: float32 [512], P('fsdp')
- grad_bias_one: float32 [512], P('fsdp')
- grad_gain_two: float32 [512], P('fsdp')
- grad_bias_two: float32 [512], P('fsdp')
- grad_gain_three: float32 [512], P('fsdp')
- grad_bias_three: float32 [512], P('fsdp')
- grad_tag_table: float32 [16, 512], P(None, 'fsdp')
Inputs may be any that keep to these rules, and one draw needn't show every extreme that they name: `seg_ids`: numbers never fall along a sequence; every number 0 to 15 is used; a sentence has 1 to 256 positions, one exactly 256.
All inputs are finite; a program needn't handle non-finite values. No bound on the sum of `keep_mask` on one device may be relied on, other than what follows from the above.
Results may differ from a plain program's by a relative error of at most 0.028.
Values may be sent and summed in bfloat16 or wider, within the bound.
No kernel may reach another device: no remote copies, remote signals or barrier semaphores. Data moves between devices by JAX's collectives and lax.ppermute only.
A program may use at most 192 MiB of HBM per device.

v0:
```python
import jax
import jax.numpy as jnp
from jax import lax
from jax.sharding import PartitionSpec as P

HEADS = 8
HEAD_DIM = 64
MAXLEN = 256


EPSILON = 1e-05
HIGHEST = lax.Precision.HIGHEST


def shifted(shard, axis, by):
    size = lax.axis_size(axis)
    pairs = [(i, i + by) for i in range(size) if 0 <= i + by < size]
    return lax.ppermute(shard, axis, pairs)


def with_halo(cells, sides, width):
    for axis, dim in sides:
        count = lax.axis_size(axis)
        ends = count - 1
        head = lax.slice_in_dim(cells, 0, width, axis=dim)
        tail = lax.slice_in_dim(cells, cells.shape[dim] - width, cells.shape[dim], axis=dim)
        cells = jnp.concatenate(
            [
                lax.ppermute(tail, axis, [(i, (i + 1) % count) for i in range(ends)]),
                cells,
                lax.ppermute(head, axis, [((i + 1) % count, i) for i in range(ends)]),
            ],
            axis=dim,
        )
    return cells


def dot_plain(left, right):
    return jnp.dot(left, right, preferred_element_type=jnp.float32)


def dot_first(left, right):
    return lax.dot_general(
        left, right, (((0,), (0,)), ((), ())), preferred_element_type=jnp.float32
    )


def dot_second(left, right):
    return lax.dot_general(
        left, right, (((1,), (1,)), ((), ())), preferred_element_type=jnp.float32
    )


def norm_forward(values_in, gain_vec, bias_vec):
    center = values_in - jnp.mean(values_in, -1, keepdims=True)
    inverse = lax.rsqrt(jnp.mean(center * center, -1, keepdims=True) + EPSILON)
    unit_rows = center * inverse
    return (unit_rows * gain_vec + bias_vec, unit_rows, inverse)


def norm_backward(grad_rows, unit_rows, inverse, gain_vec):
    scaled = grad_rows * gain_vec
    centered = (
        scaled
        - jnp.mean(scaled, -1, keepdims=True)
        - unit_rows * jnp.mean(scaled * unit_rows, -1, keepdims=True)
    )
    return (inverse * centered, jnp.sum(grad_rows * unit_rows, 0), jnp.sum(grad_rows, 0))


def lookup(small_table, row_index):
    matches = row_index[:, None] == jnp.arange(small_table.shape[0], dtype=jnp.int32)[None, :]
    return jnp.sum(jnp.where(matches, small_table[None, :], 0), 1)


def window_mask(row_meta, first_row, row_count, key_count, crossing):
    base_row, seg_pad, keep_pad, seg_rows, span_lower, span_upper = row_meta
    query_pos = base_row + first_row + jnp.arange(row_count, dtype=jnp.int32)
    key_pos = base_row + first_row - MAXLEN + jnp.arange(key_count, dtype=jnp.int32)
    if crossing:
        return (key_pos[None, :] >= span_lower[:, None]) & (key_pos[None, :] < span_upper[:, None])
    key_seg = lax.dynamic_slice_in_dim(seg_pad, base_row + first_row, key_count, 0)
    key_keep = lax.dynamic_slice_in_dim(keep_pad, base_row + first_row, key_count, 0)
    same_seg = key_seg[None, :] == seg_rows[:, None]
    causal = key_pos[None, :] <= query_pos[:, None]
    visible = (key_keep[None, :] == 1) | (key_pos[None, :] == query_pos[:, None])
    return same_seg & causal & visible


def block_scores(query_blk, key_win, allowed):
    heads_q = query_blk.reshape(query_blk.shape[0], HEADS, HEAD_DIM)
    heads_k = key_win.reshape(key_win.shape[0], HEADS, HEAD_DIM)
    scores = jnp.einsum(
        "rhd,whd->hrw", heads_q, heads_k, preferred_element_type=jnp.float32
    ) * HEAD_DIM ** (-0.5)
    return jnp.where(allowed[None], scores, -1e30)


def attend_forward(queries, key_ext, value_ext, row_meta, crossing):
    local_rows = queries.shape[0]
    block_rows = min(512, local_rows)
    extra_rows = 2 * MAXLEN if crossing else MAXLEN
    key_count = block_rows + extra_rows
    allowed = window_mask(row_meta, 0, block_rows, key_count, crossing)
    scores = block_scores(queries, key_ext, allowed)
    highest = jnp.max(scores, -1, keepdims=True)
    exponent = jnp.exp(scores - highest)
    row_total = jnp.sum(exponent, -1, keepdims=True)
    weights = (exponent / row_total).astype(jnp.bfloat16)
    heads_v = value_ext.reshape(key_count, HEADS, HEAD_DIM)
    mixed_out = jnp.einsum("hrw,whd->rhd", weights, heads_v, preferred_element_type=jnp.float32)
    pieces = mixed_out.reshape(block_rows, HEADS * HEAD_DIM)
    log_totals = [highest + jnp.log(row_total)]
    return (pieces, log_totals)


def attend_backward(queries, key_ext, value_ext, row_meta, crossing, log_totals, grad_mixed):
    local_rows = queries.shape[0]
    block_rows = min(512, local_rows)
    extra_rows = 2 * MAXLEN if crossing else MAXLEN
    key_count = block_rows + extra_rows
    scale = HEAD_DIM ** (-0.5)
    grad_queries = []
    grad_keys = jnp.zeros(key_ext.shape, jnp.float32)
    grad_values = jnp.zeros(value_ext.shape, jnp.float32)
    for block_number, first_row in enumerate(range(0, local_rows, block_rows)):
        allowed = window_mask(row_meta, first_row, block_rows, key_count, crossing)
        scores = block_scores(queries, key_ext, allowed)
        weights = jnp.exp(scores - log_totals[block_number])
        heads_q = queries.reshape(block_rows, HEADS, HEAD_DIM)
        heads_k = key_ext.reshape(key_count, HEADS, HEAD_DIM)
        heads_v = value_ext.reshape(key_count, HEADS, HEAD_DIM)
        heads_g = grad_mixed.reshape(block_rows, HEADS, HEAD_DIM)
        grad_weights = jnp.einsum(
            "rhd,whd->hrw", heads_g, heads_v, preferred_element_type=jnp.float32
        )
        centre = jnp.sum(grad_weights * weights, -1, keepdims=True)
        grad_scores = (weights * (grad_weights - centre)).astype(jnp.bfloat16)
        grad_query_blk = (
            jnp.einsum("hrw,whd->rhd", grad_scores, heads_k, preferred_element_type=jnp.float32)
            * scale
        )
        grad_key_blk = (
            jnp.einsum("hrw,rhd->whd", grad_scores, heads_q, preferred_element_type=jnp.float32)
            * scale
        )
        grad_value_blk = jnp.einsum(
            "hrw,rhd->whd",
            weights.astype(jnp.bfloat16),
            heads_g,
            preferred_element_type=jnp.float32,
        )
        grad_queries.append(grad_query_blk.reshape(block_rows, HEADS * HEAD_DIM))
        grad_keys = grad_keys.at[first_row : first_row + key_count].add(
            grad_key_blk.reshape(key_count, HEADS * HEAD_DIM)
        )
        grad_values = grad_values.at[first_row : first_row + key_count].add(
            grad_value_blk.reshape(key_count, HEADS * HEAD_DIM)
        )
    return (grad_queries[0], grad_keys, grad_values)


def on_device(
    inputs,
    encoded,
    cotangent,
    seg_ids,
    keep_mask,
    pair_tags,
    cut_lo,
    cut_hi,
    w_query,
    w_key,
    w_value,
    w_out,
    c_query,
    c_key,
    c_value,
    c_out,
    w_up,
    w_down,
    gain_one,
    bias_one,
    gain_two,
    bias_two,
    gain_three,
    bias_three,
    tag_table,
):
    local_rows = inputs.shape[1]
    base_row = lax.axis_index("seq") * local_rows
    tag_count = tag_table.shape[0]

    def fetch_weights():
        return (
            lax.all_gather(w_query, "fsdp", axis=0, tiled=True),
            lax.all_gather(w_key, "fsdp", axis=0, tiled=True),
            lax.all_gather(w_value, "fsdp", axis=0, tiled=True),
            lax.all_gather(w_out, "fsdp", axis=0, tiled=True),
            lax.all_gather(c_query, "fsdp", axis=0, tiled=True),
            lax.all_gather(c_key, "fsdp", axis=0, tiled=True),
            lax.all_gather(c_value, "fsdp", axis=0, tiled=True),
            lax.all_gather(c_out, "fsdp", axis=0, tiled=True),
            lax.all_gather(w_up, "fsdp", axis=0, tiled=True),
            lax.all_gather(w_down, "fsdp", axis=0, tiled=True),
            lax.all_gather(gain_one, "fsdp", axis=0, tiled=True),
            lax.all_gather(bias_one, "fsdp", axis=0, tiled=True),
            lax.all_gather(gain_two, "fsdp", axis=0, tiled=True),
            lax.all_gather(bias_two, "fsdp", axis=0, tiled=True),
            lax.all_gather(gain_three, "fsdp", axis=0, tiled=True),
            lax.all_gather(bias_three, "fsdp", axis=0, tiled=True),
            lax.all_gather(tag_table, "fsdp", axis=1, tiled=True),
        )

    totals = []
    layer_outs = []
    input_grads = []
    encoder_grads = []
    for micro_index in range(inputs.shape[0]):
        seg_full = seg_ids[micro_index]
        seg_rows = lax.dynamic_slice_in_dim(seg_full, base_row, local_rows, 0)
        seg_starts = jnp.searchsorted(seg_full, seg_rows, side="left")
        seg_ends = jnp.searchsorted(seg_full, seg_rows, side="right")
        half_len = (seg_ends - seg_starts - 1) // 2
        span_lower = seg_starts + jnp.minimum(lookup(cut_lo[micro_index], seg_rows), half_len)
        span_upper = seg_ends - jnp.minimum(lookup(cut_hi[micro_index], seg_rows), half_len)
        tag_rows = lookup(pair_tags[micro_index], seg_rows)
        seg_pad = jnp.pad(seg_full, MAXLEN, constant_values=-1)
        keep_pad = jnp.pad(keep_mask[micro_index], MAXLEN)
        row_meta = (base_row, seg_pad, keep_pad, seg_rows, span_lower, span_upper)
        tag_match = tag_rows[:, None] == jnp.arange(tag_count, dtype=jnp.int32)[None, :]
        full_weights = fetch_weights()
        (
            f_query,
            f_key,
            f_value,
            f_out,
            f_cquery,
            f_ckey,
            f_cvalue,
            f_cout,
            f_up,
            f_down,
            f_gain_one,
            f_bias_one,
            f_gain_two,
            f_bias_two,
            f_gain_three,
            f_bias_three,
            f_tags,
        ) = full_weights
        start = inputs[micro_index].astype(jnp.float32) + dot_plain(
            tag_match.astype(jnp.bfloat16), f_tags
        )
        start_low = start.astype(jnp.bfloat16)
        queries = dot_plain(start_low, f_query).astype(jnp.bfloat16)
        keys = dot_plain(start_low, f_key).astype(jnp.bfloat16)
        values = dot_plain(start_low, f_value).astype(jnp.bfloat16)
        rim_pair = shifted(jnp.stack([keys, values]), "seq", 1)
        key_ext = jnp.concatenate([rim_pair[0], keys], 0)
        value_ext = jnp.concatenate([rim_pair[1], values], 0)
        self_mix_f, self_logs = attend_forward(queries, key_ext, value_ext, row_meta, False)
        self_mix = self_mix_f.astype(jnp.bfloat16)
        normed_one, unit_one, inverse_one = norm_forward(
            start + dot_plain(self_mix, f_out),
            f_gain_one.astype(jnp.float32),
            f_bias_one.astype(jnp.float32),
        )
        normed_one_low = normed_one.astype(jnp.bfloat16)
        cross_queries = dot_plain(normed_one_low, f_cquery).astype(jnp.bfloat16)
        encoded_now = encoded[micro_index]
        enc_pair = jnp.stack(
            [
                dot_plain(encoded_now, f_ckey).astype(jnp.bfloat16),
                dot_plain(encoded_now, f_cvalue).astype(jnp.bfloat16),
            ]
        )
        enc_ext = with_halo(enc_pair, (("seq", 1),), MAXLEN)
        cross_mix_f, cross_logs = attend_forward(
            cross_queries, enc_ext[0], enc_ext[1], row_meta, True
        )
        cross_mix = cross_mix_f.astype(jnp.bfloat16)
        normed_two, unit_two, inverse_two = norm_forward(
            normed_one + dot_plain(cross_mix, f_cout),
            f_gain_two.astype(jnp.float32),
            f_bias_two.astype(jnp.float32),
        )
        normed_two_low = normed_two.astype(jnp.bfloat16)
        hidden = dot_plain(normed_two_low, f_up)
        gelu_out, gelu_pull = jax.vjp(jax.nn.gelu, hidden)
        activated = gelu_out.astype(jnp.bfloat16)
        gain_last = f_gain_three.astype(jnp.float32)
        result, unit_three, inverse_three = norm_forward(
            normed_two + dot_plain(activated, f_down), gain_last, f_bias_three.astype(jnp.float32)
        )
        layer_outs.append(result.astype(jnp.bfloat16))
        back_weights = fetch_weights()
        (
            b_query,
            b_key,
            b_value,
            b_out,
            b_cquery,
            b_ckey,
            b_cvalue,
            b_cout,
            b_up,
            b_down,
            b_gain_one,
            b_bias_one,
            b_gain_two,
            b_bias_two,
            b_gain_three,
            b_bias_three,
            b_tags,
        ) = back_weights
        d_three, g_gain_three, g_bias_three = norm_backward(
            cotangent[micro_index].astype(jnp.float32),
            unit_three,
            inverse_three,
            b_gain_three.astype(jnp.float32),
        )
        d_feed = d_three.astype(jnp.bfloat16)
        g_down = dot_first(activated, d_feed)
        d_hidden = gelu_pull(dot_second(d_feed, b_down))[0].astype(jnp.bfloat16)
        g_up = dot_first(normed_two_low, d_hidden)
        d_two, g_gain_two, g_bias_two = norm_backward(
            d_three + dot_second(d_hidden, b_up),
            unit_two,
            inverse_two,
            b_gain_two.astype(jnp.float32),
        )
        d_cross_branch = d_two.astype(jnp.bfloat16)
        g_cout = dot_first(cross_mix, d_cross_branch)
        d_cross_mix = dot_second(d_cross_branch, b_cout).astype(jnp.bfloat16)
        d_cq, d_ck_ext, d_cv_ext = attend_backward(
            cross_queries, enc_ext[0], enc_ext[1], row_meta, True, cross_logs, d_cross_mix
        )
        edges = jnp.stack(
            [
                jnp.concatenate([d_ck_ext[:MAXLEN], d_ck_ext[-MAXLEN:]], 0),
                jnp.concatenate([d_cv_ext[:MAXLEN], d_cv_ext[-MAXLEN:]], 0),
            ]
        )
        arrived = with_halo(edges.astype(jnp.bfloat16), (("seq", 1),), MAXLEN).astype(edges.dtype)
        d_enc_pair = jnp.stack(
            [d_ck_ext[MAXLEN : MAXLEN + local_rows], d_cv_ext[MAXLEN : MAXLEN + local_rows]]
        )
        d_enc_pair = d_enc_pair.at[:, :MAXLEN].add(arrived[:, :MAXLEN])
        d_enc_pair = d_enc_pair.at[:, local_rows - MAXLEN :].add(arrived[:, 3 * MAXLEN :])
        d_enc_low = d_enc_pair.astype(jnp.bfloat16)
        g_ckey = dot_first(encoded_now, d_enc_low[0])
        g_cvalue = dot_first(encoded_now, d_enc_low[1])
        encoder_grads.append(
            (dot_second(d_enc_low[0], b_ckey) + dot_second(d_enc_low[1], b_cvalue)).astype(
                jnp.bfloat16
            )
        )
        d_cq_low = d_cq.astype(jnp.bfloat16)
        g_cquery = dot_first(normed_one_low, d_cq_low)
        d_one, g_gain_one, g_bias_one = norm_backward(
            d_two + dot_second(d_cq_low, b_cquery),
            unit_one,
            inverse_one,
            b_gain_one.astype(jnp.float32),
        )
        d_self_branch = d_one.astype(jnp.bfloat16)
        g_out = dot_first(self_mix, d_self_branch)
        d_self_mix = dot_second(d_self_branch, b_out).astype(jnp.bfloat16)
        d_q, d_k_ext, d_v_ext = attend_backward(
            queries, key_ext, value_ext, row_meta, False, self_logs, d_self_mix
        )
        rim_back = shifted(
            jnp.stack([d_k_ext[:MAXLEN], d_v_ext[:MAXLEN]]).astype(jnp.bfloat16), "seq", -1
        ).astype(jnp.float32)
        d_keys = d_k_ext[MAXLEN:].at[local_rows - MAXLEN :].add(rim_back[0])
        d_values = d_v_ext[MAXLEN:].at[local_rows - MAXLEN :].add(rim_back[1])
        d_q_low = d_q.astype(jnp.bfloat16)
        d_k_low = d_keys.astype(jnp.bfloat16)
        d_v_low = d_values.astype(jnp.bfloat16)
        g_query = dot_first(start_low, d_q_low)
        g_key = dot_first(start_low, d_k_low)
        g_value = dot_first(start_low, d_v_low)
        d_start = (
            d_one
            + dot_second(d_q_low, b_query)
            + dot_second(d_k_low, b_key)
            + dot_second(d_v_low, b_value)
        )
        input_grads.append(d_start.astype(jnp.bfloat16))
        g_tags = lax.dot_general(
            tag_match.astype(jnp.float32),
            d_start,
            (((0,), (0,)), ((), ())),
            precision=HIGHEST,
            preferred_element_type=jnp.float32,
        )
        micro_grads = [
            g_query,
            g_key,
            g_value,
            g_out,
            g_cquery,
            g_ckey,
            g_cvalue,
            g_cout,
            g_up,
            g_down,
            g_gain_one,
            g_bias_one,
            g_gain_two,
            g_bias_two,
            g_gain_three,
            g_bias_three,
            g_tags,
        ]
        micro_grads = list(
            (
                lax.psum(
                    lax.psum_scatter(
                        micro_grads[0].astype(jnp.bfloat16), "fsdp", scatter_dimension=0, tiled=True
                    ),
                    "seq",
                ).astype(jnp.float32),
                lax.psum(
                    lax.psum_scatter(
                        micro_grads[1].astype(jnp.bfloat16), "fsdp", scatter_dimension=0, tiled=True
                    ),
                    "seq",
                ).astype(jnp.float32),
                lax.psum(
                    lax.psum_scatter(
                        micro_grads[2].astype(jnp.bfloat16), "fsdp", scatter_dimension=0, tiled=True
                    ),
                    "seq",
                ).astype(jnp.float32),
                lax.psum(
                    lax.psum_scatter(
                        micro_grads[3].astype(jnp.bfloat16), "fsdp", scatter_dimension=0, tiled=True
                    ),
                    "seq",
                ).astype(jnp.float32),
                lax.psum(
                    lax.psum_scatter(
                        micro_grads[4].astype(jnp.bfloat16), "fsdp", scatter_dimension=0, tiled=True
                    ),
                    "seq",
                ).astype(jnp.float32),
                lax.psum(
                    lax.psum_scatter(
                        micro_grads[5].astype(jnp.bfloat16), "fsdp", scatter_dimension=0, tiled=True
                    ),
                    "seq",
                ).astype(jnp.float32),
                lax.psum(
                    lax.psum_scatter(
                        micro_grads[6].astype(jnp.bfloat16), "fsdp", scatter_dimension=0, tiled=True
                    ),
                    "seq",
                ).astype(jnp.float32),
                lax.psum(
                    lax.psum_scatter(
                        micro_grads[7].astype(jnp.bfloat16), "fsdp", scatter_dimension=0, tiled=True
                    ),
                    "seq",
                ).astype(jnp.float32),
                lax.psum(
                    lax.psum_scatter(
                        micro_grads[8].astype(jnp.bfloat16), "fsdp", scatter_dimension=0, tiled=True
                    ),
                    "seq",
                ).astype(jnp.float32),
                lax.psum(
                    lax.psum_scatter(
                        micro_grads[9].astype(jnp.bfloat16), "fsdp", scatter_dimension=0, tiled=True
                    ),
                    "seq",
                ).astype(jnp.float32),
                lax.psum(
                    lax.psum_scatter(
                        micro_grads[10].astype(jnp.bfloat16),
                        "fsdp",
                        scatter_dimension=0,
                        tiled=True,
                    ),
                    "seq",
                ).astype(jnp.float32),
                lax.psum(
                    lax.psum_scatter(
                        micro_grads[11].astype(jnp.bfloat16),
                        "fsdp",
                        scatter_dimension=0,
                        tiled=True,
                    ),
                    "seq",
                ).astype(jnp.float32),
                lax.psum(
                    lax.psum_scatter(
                        micro_grads[12].astype(jnp.bfloat16),
                        "fsdp",
                        scatter_dimension=0,
                        tiled=True,
                    ),
                    "seq",
                ).astype(jnp.float32),
                lax.psum(
                    lax.psum_scatter(
                        micro_grads[13].astype(jnp.bfloat16),
                        "fsdp",
                        scatter_dimension=0,
                        tiled=True,
                    ),
                    "seq",
                ).astype(jnp.float32),
                lax.psum(
                    lax.psum_scatter(
                        micro_grads[14].astype(jnp.bfloat16),
                        "fsdp",
                        scatter_dimension=0,
                        tiled=True,
                    ),
                    "seq",
                ).astype(jnp.float32),
                lax.psum(
                    lax.psum_scatter(
                        micro_grads[15].astype(jnp.bfloat16),
                        "fsdp",
                        scatter_dimension=0,
                        tiled=True,
                    ),
                    "seq",
                ).astype(jnp.float32),
                lax.psum(
                    lax.psum_scatter(
                        micro_grads[16].astype(jnp.bfloat16),
                        "fsdp",
                        scatter_dimension=1,
                        tiled=True,
                    ),
                    "seq",
                ).astype(jnp.float32),
            )
        )
        if micro_index == 0:
            totals = micro_grads
        else:
            totals = [
                first_term + second_term for first_term, second_term in zip(totals, micro_grads)
            ]
    return (
        jnp.stack(layer_outs),
        jnp.stack(input_grads),
        jnp.stack(encoder_grads),
        totals[0],
        totals[1],
        totals[2],
        totals[3],
        totals[4],
        totals[5],
        totals[6],
        totals[7],
        totals[8],
        totals[9],
        totals[10],
        totals[11],
        totals[12],
        totals[13],
        totals[14],
        totals[15],
        totals[16],
    )


def solution(mesh):
    in_specs = (
        P("fsdp", "seq", None),
        P("fsdp", "seq", None),
        P("fsdp", "seq", None),
        P("fsdp", None),
        P("fsdp", None),
        P("fsdp", None),
        P("fsdp", None),
        P("fsdp", None),
        P("fsdp", None),
        P("fsdp", None),
        P("fsdp", None),
        P("fsdp", None),
        P("fsdp", None),
        P("fsdp", None),
        P("fsdp", None),
        P("fsdp", None),
        P("fsdp", None),
        P("fsdp", None),
        P("fsdp"),
        P("fsdp"),
        P("fsdp"),
        P("fsdp"),
        P("fsdp"),
        P("fsdp"),
        P(None, "fsdp"),
    )
    out_specs = (
        P("fsdp", "seq", None),
        P("fsdp", "seq", None),
        P("fsdp", "seq", None),
        P("fsdp", None),
        P("fsdp", None),
        P("fsdp", None),
        P("fsdp", None),
        P("fsdp", None),
        P("fsdp", None),
        P("fsdp", None),
        P("fsdp", None),
        P("fsdp", None),
        P("fsdp", None),
        P("fsdp"),
        P("fsdp"),
        P("fsdp"),
        P("fsdp"),
        P("fsdp"),
        P("fsdp"),
        P(None, "fsdp"),
    )
    return jax.shard_map(
        on_device, mesh=mesh, in_specs=in_specs, out_specs=out_specs, check_vma=False
    )
```

profile of v0, /device:TPU:0, one launch (start us, length us, event | category | flops | bytes accessed | tf_op | source)
XLA Modules:
  0.0 1132.4 jit_solution(4239963321983547007)
XLA Ops:
  7.2 17.7 %all_gather.41 = bf16[512,512]{1,0:T(8,128)(2,1)S(1)} all-gather(bf16[128,512]{1,0:T(8,128)(2,1)} %param.110), channel_id=1, replica_groups=mesh['seq'=8,'fsdp'=4] {'fsdp'}, dimensions={0}, use_global_device_ids=true | all-gather | bytes 655360 | tf_op jit(solution)/shard_map/all_gather | solution.py:201
  25.0 16.6 %all_gather.42 = bf16[512,512]{1,0:T(8,128)(2,1)S(1)} all-gather(bf16[128,512]{1,0:T(8,128)(2,1)} %param.111), channel_id=1, replica_groups=mesh['seq'=8,'fsdp'=4] {'fsdp'}, dimensions={0}, use_global_device_ids=true | all-gather | bytes 655360 | tf_op jit(solution)/shard_map/all_gather | solution.py:202
  45.6 3.8 collective-permute-start.4
  52.3 3.8 collective-permute-start.1
  56.1 12.1 %all_gather.34 = bf16[16,512]{1,0:T(8,128)(2,1)S(1)} all-gather(bf16[16,128]{1,0:T(8,128)(2,1)S(1)} %copy-done.158), channel_id=1, replica_groups=mesh['seq'=8,'fsdp'=4] {'fsdp'}, dimensions={1}, use_global_device_ids=true | all-gather | bytes 20480 | tf_op jit(solution)/shard_map/all_gather | solution.py:212
  68.5 21.6 %all_gather.35 = bf16[512,512]{1,0:T(8,128)(2,1)S(1)} all-gather(bf16[128,512]{1,0:T(8,128)(2,1)S(1)} %copy-done.134), channel_id=1, replica_groups=mesh['seq'=8,'fsdp'=4] {'fsdp'}, dimensions={0}, use_global_device_ids=true | all-gather | bytes 655360 | tf_op jit(solution)/shard_map/all_gather | solution.py:197
  90.0 21.6 %all_gather.36 = bf16[512,512]{1,0:T(8,128)(2,1)S(1)} all-gather(bf16[128,512]{1,0:T(8,128)(2,1)S(1)} %copy-done.135), channel_id=1, replica_groups=mesh['seq'=8,'fsdp'=4] {'fsdp'}, dimensions={0}, use_global_device_ids=true | all-gather | bytes 655360 | tf_op jit(solution)/shard_map/all_gather | solution.py:198
  120.0 19.8 %all_gather.37 = bf16[512,512]{1,0:T(8,128)(2,1)S(1)} all-gather(bf16[128,512]{1,0:T(8,128)(2,1)S(1)} %copy-done.136), channel_id=1, replica_groups=mesh['seq'=8,'fsdp'=4] {'fsdp'}, dimensions={0}, use_global_device_ids=true | all-gather | bytes 655360 | tf_op jit(solution)/shard_map/all_gather | solution.py:196
  141.0 10.8 all-gather
  151.8 7.6 all-gather.1
  159.4 10.2 all-gather.2
  169.6 7.5 all-gather.3
  177.1 9.5 all-gather.4
  186.6 7.5 all-gather.5
  194.1 21.8 %while.107 = (s32[]{:T(128)}, u32[256]{0:T(256)S(1)}, u32[256]{0:T(256)S(1)}, s32[2048]{0:T(1024)S(1)}, s32[256]{0:T(256)S(1)}, /*index=5*/s32[]{:T(128)}, s32[]{:T(128)}, s32[]{}) while((s32[]{:T(128)}, u32[256]{0:T(256)S(1)}, u32[256]{0:T(256)S(1)}, s32[2048]{0:T(1024)S(1)}, s32[256]{0:T(256)S(1)}, /*index=5*/s32[]{:T(128)}, ...), condition=%wide.region_9.10_spmd.clone, body=%wide.region_8.9_spmd.clone.sunk | while | flops 5636 | bytes 22125 | solution.py:223
  216.0 21.8 %while.106 = (s32[]{:T(128)}, u32[256]{0:T(256)S(1)}, u32[256]{0:T(256)S(1)}, s32[2048]{0:T(1024)S(1)}, s32[256]{0:T(256)S(1)}, /*index=5*/s32[]{:T(128)}, s32[]{:T(128)}, s32[]{}) while((s32[]{:T(128)}, u32[256]{0:T(256)S(1)}, u32[256]{0:T(256)S(1)}, s32[2048]{0:T(1024)S(1)}, s32[256]{0:T(256)S(1)}, /*index=5*/s32[]{:T(128)}, ...), condition=%wide.region_6.7_spmd.clone, body=%wide.region_5.6_spmd.clone.sunk | while | flops 5636 | bytes 22125 | solution.py:222
  237.9 21.8 %while.109 = (s32[]{:T(128)}, u32[256]{0:T(256)S(1)}, u32[256]{0:T(256)S(1)}, s32[2048]{0:T(1024)S(1)}, s32[256]{0:T(256)S(1)}, /*index=5*/s32[]{:T(128)}, s32[]{:T(128)}, s32[]{}) while((s32[]{:T(128)}, u32[256]{0:T(256)S(1)}, u32[256]{0:T(256)S(1)}, s32[2048]{0:T(1024)S(1)}, s32[256]{0:T(256)S(1)}, /*index=5*/s32[]{:T(128)}, ...), condition=%wide.region_26.27_spmd.clone, body=%wide.region_25.26_spmd.clone.sunk | while | flops 5636 | bytes 22125 | solution.py:223
  259.7 21.8 %while.108 = (s32[]{:T(128)}, u32[256]{0:T(256)S(1)}, u32[256]{0:T(256)S(1)}, s32[2048]{0:T(1024)S(1)}, s32[256]{0:T(256)S(1)}, /*index=5*/s32[]{:T(128)}, s32[]{:T(128)}, s32[]{}) while((s32[]{:T(128)}, u32[256]{0:T(256)S(1)}, u32[256]{0:T(256)S(1)}, s32[2048]{0:T(1024)S(1)}, s32[256]{0:T(256)S(1)}, /*index=5*/s32[]{:T(128)}, ...), condition=%wide.region_23.24_spmd.clone, body=%wide.region_22.23_spmd.clone.sunk | while | flops 5636 | bytes 22125 | solution.py:222
  281.6 16.3 %all_gather.38 = bf16[512,512]{1,0:T(8,128)(2,1)S(1)} all-gather(bf16[128,512]{1,0:T(8,128)(2,1)S(1)} %copy-done.137), channel_id=1, replica_groups=mesh['seq'=8,'fsdp'=4] {'fsdp'}, dimensions={0}, use_global_device_ids=true | all-gather | bytes 655360 | tf_op jit(solution)/shard_map/all_gather | solution.py:199
  297.9 15.9 %all_gather.43 = bf16[512,512]{1,0:T(8,128)(2,1)S(1)} all-gather(bf16[128,512]{1,0:T(8,128)(2,1)S(1)} %copy-done.138), channel_id=1, replica_groups=mesh['seq'=8,'fsdp'=4] {'fsdp'}, dimensions={0}, use_global_device_ids=true | all-gather | bytes 655360 | tf_op jit(solution)/shard_map/all_gather | solution.py:200
  318.4 14.7 %all_gather.44 = bf16[512,512]{1,0:T(8,128)(2,1)S(1)} all-gather(bf16[128,512]{1,0:T(8,128)(2,1)S(1)} %copy-done.139), channel_id=1, replica_groups=mesh['seq'=8,'fsdp'=4] {'fsdp'}, dimensions={0}, use_global_device_ids=true | all-gather | bytes 655360 | tf_op jit(solution)/shard_map/all_gather | solution.py:203
  408.7 5.6 fusion.207
  420.4 5.5 multiply_convert_fusion.1
  456.5 5.7 collective-permute-start.10
  495.8 4.1 fusion.52
  502.8 4.0 multiply_convert_fusion.3
  517.5 4.0 multiply_reduce_fusion.2
  537.5 8.4 collective-permute-done.7
  548.7 4.2 convolution_convert_fusion.1
  553.9 4.2 convolution_convert_fusion
  566.4 17.2 %all-reduce.18 = (bf16[512]{0:T(512)(128)(2,1)S(1)}, bf16[512]{0:T(512)(128)(2,1)S(1)}, bf16[512]{0:T(512)(128)(2,1)S(1)}, bf16[512]{0:T(512)(128)(2,1)S(1)}, bf...) all-reduce(bf16[512]{0:T(512)(128)(2,1)S(1)} %get-tuple-element.746, ...), channel_id=23, replica_groups=mesh['seq'=8,'fsdp'=4] {'fsdp'}, use_global_device_ids=true, to_apply=%region_94.95.clone | all-reduce | flops 6144 | bytes 24576
  602.0 19.7 %reduce-scatter.53.cloned.1.call-done = bf16[128,512]{1,0:T(8,128)(2,1)} async-done(((bf16[512,512]{1,0:T(8,128)(2,1)}), bf16[128,512]{1,0:T(8,128)(2,1)}) %reduce-scatter.53.cloned.1.call-update) | async-done | bytes 131088 | tf_op jit(solution)/shard_map/reduce_scatter | solution.py:444
  621.7 22.3 %reduce-scatter.49.cloned.1.call-done = bf16[128,512]{1,0:T(8,128)(2,1)} async-done(((bf16[512,512]{1,0:T(8,128)(2,1)}), bf16[128,512]{1,0:T(8,128)(2,1)}) %reduce-scatter.49.cloned.1.call-update) | async-done | bytes 131088 | tf_op jit(solution)/shard_map/reduce_scatter | solution.py:438
  643.9 22.1 %reduce-scatter.47.cloned.1.call-done = bf16[128,512]{1,0:T(8,128)(2,1)} async-done(((bf16[512,512]{1,0:T(8,128)(2,1)}), bf16[128,512]{1,0:T(8,128)(2,1)}) %reduce-scatter.47.cloned.1.call-update) | async-done | bytes 131088 | tf_op jit(solution)/shard_map/reduce_scatter | solution.py:438
  666.0 22.2 %reduce-scatter.35.cloned.1.call-done = bf16[128,512]{1,0:T(8,128)(2,1)} async-done(((bf16[512,512]{1,0:T(8,128)(2,1)}), bf16[128,512]{1,0:T(8,128)(2,1)}) %reduce-scatter.35.cloned.1.call-update) | async-done | bytes 131088 | tf_op jit(solution)/shard_map/reduce_scatter | solution.py:420
  688.3 22.1 %reduce-scatter.37.cloned.1.call-done = bf16[128,512]{1,0:T(8,128)(2,1)} async-done(((bf16[512,512]{1,0:T(8,128)(2,1)}), bf16[128,512]{1,0:T(8,128)(2,1)}) %reduce-scatter.37.cloned.1.call-update) | async-done | bytes 131088 | tf_op jit(solution)/shard_map/reduce_scatter | solution.py:420
  710.4 22.0 %reduce-scatter.39.cloned.1.call-done = bf16[128,512]{1,0:T(8,128)(2,1)} async-done(((bf16[512,512]{1,0:T(8,128)(2,1)}), bf16[128,512]{1,0:T(8,128)(2,1)}) %reduce-scatter.39.cloned.1.call-update) | async-done | bytes 131088 | tf_op jit(solution)/shard_map/reduce_scatter | solution.py:426
  732.4 22.1 %reduce-scatter.43.cloned.1.call-done = bf16[128,512]{1,0:T(8,128)(2,1)} async-done(((bf16[512,512]{1,0:T(8,128)(2,1)}), bf16[128,512]{1,0:T(8,128)(2,1)}) %reduce-scatter.43.cloned.1.call-update) | async-done | bytes 131088 | tf_op jit(solution)/shard_map/reduce_scatter | solution.py:432
  754.5 22.6 %reduce-scatter.41.cloned.1.call-done = bf16[128,512]{1,0:T(8,128)(2,1)} async-done(((bf16[512,512]{1,0:T(8,128)(2,1)}), bf16[128,512]{1,0:T(8,128)(2,1)}) %reduce-scatter.41.cloned.1.call-update) | async-done | bytes 131088 | tf_op jit(solution)/shard_map/reduce_scatter | solution.py:426
  777.1 22.0 %reduce-scatter.45.cloned.1.call-done = bf16[128,512]{1,0:T(8,128)(2,1)} async-done(((bf16[512,512]{1,0:T(8,128)(2,1)}), bf16[128,512]{1,0:T(8,128)(2,1)}) %reduce-scatter.45.cloned.1.call-update) | async-done | bytes 131088 | tf_op jit(solution)/shard_map/reduce_scatter | solution.py:432
  799.1 44.4 %reduce-scatter.63.cloned.1.call-done = bf16[512,512]{1,0:T(8,128)(2,1)} async-done(((bf16[2048,512]{1,0:T(8,128)(2,1)}), bf16[512,512]{1,0:T(8,128)(2,1)}) %reduce-scatter.63.cloned.1.call-update) | async-done | bytes 524304 | tf_op jit(solution)/shard_map/reduce_scatter | solution.py:474
  843.6 45.5 %reduce-scatter.65.cloned.1.call-done = bf16[512,512]{1,0:T(8,128)(2,1)} async-done(((bf16[2048,512]{1,0:T(8,128)(2,1)}), bf16[512,512]{1,0:T(8,128)(2,1)}) %reduce-scatter.65.cloned.1.call-update) | async-done | bytes 524304 | tf_op jit(solution)/shard_map/reduce_scatter | solution.py:474
  889.0 45.5 %reduce-scatter.61.cloned.1.call-done = bf16[128,2048]{1,0:T(8,128)(2,1)} async-done(((bf16[512,2048]{1,0:T(8,128)(2,1)}), bf16[128,2048]{1,0:T(8,128)(2,1)}) %reduce-scatter.61.cloned.1.call-update) | async-done | bytes 524304 | tf_op jit(solution)/shard_map/reduce_scatter | solution.py:468
  934.6 45.6 %reduce-scatter.59.cloned.1.call-done = bf16[128,2048]{1,0:T(8,128)(2,1)} async-done(((bf16[512,2048]{1,0:T(8,128)(2,1)}), bf16[128,2048]{1,0:T(8,128)(2,1)}) %reduce-scatter.59.cloned.1.call-update) | async-done | bytes 524304 | tf_op jit(solution)/shard_map/reduce_scatter | solution.py:468
  983.3 18.2 %reduce-scatter.75.cloned.1.call-done = bf16[128,16]{1,0:T(8,128)(2,1)} async-done(((bf16[512,16]{1,0:T(8,128)(2,1)}), bf16[128,16]{1,0:T(8,128)(2,1)}) %reduce-scatter.75.cloned.1.call-update) | async-done | bytes 4112
  1002.3 19.4 %reduce-scatter.77.cloned.1.call-done = bf16[128,16]{1,0:T(8,128)(2,1)} async-done(((bf16[512,16]{1,0:T(8,128)(2,1)}), bf16[128,16]{1,0:T(8,128)(2,1)}) %reduce-scatter.77.cloned.1.call-update) | async-done | bytes 4112
  1022.5 23.1 %all-reduce.16 = (bf16[128]{0:T(256)(128)(2,1)S(1)}, bf16[128]{0:T(256)(128)(2,1)S(1)}, bf16[128]{0:T(256)(128)(2,1)S(1)}, bf16[128]{0:T(256)(128)(2,1)S(1)}, bf...) all-reduce(bf16[128]{0:T(256)(128)(2,1)S(1)} %dynamic-slice.85, ...), channel_id=1, replica_groups=mesh['seq'=8,'fsdp'=4] {'seq'}, use_global_device_ids=true, to_apply=%region_95.96 | all-reduce | flops 5632 | bytes 22528 | tf_op jit(solution)/shard_map/psum | solution.py:479
  1049.3 65.5 %all-reduce.21.cloned.1.call-done = (bf16[128,512]{1,0:T(8,128)(2,1)}, bf16[128,512]{1,0:T(8,128)(2,1)}, bf16[128,512]{1,0:T(8,128)(2,1)}, bf16[128,512]{1,0:T(8...) async-done(((bf16[128,512]{1,0:T(8,128)(2,1)}, ...) | async-done | bytes 4194320 | tf_op jit(solution)/shard_map/psum | solution.py:419
  (1014 shorter events, 327.3 us)
Async XLA Ops:
  7.2 376.8 %all-gather.9.cloned.1.call-start = ((), (), s32[]{:S(2)}) async-start(), calls=%async_computation.22 | async-start | bytes 2621440 | tf_op jit(solution)/shard_map/all_gather | solution.py:204
  44.1 45.9 %copy-start.135 = (bf16[128,512]{1,0:T(8,128)(2,1)S(1)}, bf16[128,512]{1,0:T(8,128)(2,1)}, u32[]{:S(2)}) copy-start(bf16[128,512]{1,0:T(8,128)(2,1)} %param.107) | copy-start | bytes 393220
  44.1 290.9 %collective-permute-start.5 = (bf16[2,256,512]{2,1,0:T(8,128)(2,1)}, bf16[2,256,512]{2,1,0:T(8,128)(2,1)}, u32[]{:S(2)}, u32[]{:S(2)}) collective-permute-start(bf16[2,256,512]{2,1,0:T(8,128)(2,1)} %pad_maximum_fusion.17), channel_id=1, source_target_pairs={{4,0},{8,4},{12,8},{16,12},{20,16},{24,20},{28,24},{5,1},{9,5},{13... | collective-permute-start | bytes 1572872 | tf_op jit(solution)/shard_map/ppermute | solution.py:31
  45.6 291.5 %collective-permute-start.4 = (bf16[2,256,512]{2,1,0:T(8,128)(2,1)}, bf16[2,256,512]{2,1,0:T(8,128)(2,1)}, u32[]{:S(2)}, u32[]{:S(2)}) collective-permute-start(bf16[2,256,512]{2,1,0:T(8,128)(2,1)} %pad_maximum_fusion.17), channel_id=1, source_target_pairs={{0,4},{4,8},{8,12},{12,16},{16,20},{20,24},{24,28},{1,5},{5,9},{9,... | collective-permute-start | bytes 1572872 | tf_op jit(solution)/shard_map/ppermute | solution.py:29
  49.4 62.2 %copy-start.127 = (bf16[2,256,512]{2,1,0:T(8,128)(2,1)S(1)}, bf16[2,256,512]{2,1,0:T(8,128)(2,1)}, u32[]{:S(2)}) copy-start(bf16[2,256,512]{2,1,0:T(8,128)(2,1)} %param.97) | copy-start | bytes 1572868
  49.4 338.7 %all-gather.11.cloned.1.call-start = ((), (), s32[]{:S(2)}) async-start(), calls=%async_computation.23 | async-start | bytes 2621440 | tf_op jit(solution)/shard_map/all_gather | solution.py:205
  49.8 62.9 %copy-start.74 = (bf16[1,256,512]{2,1,0:T(8,128)(2,1)}, bf16[1,256,512]{2,1,0:T(8,128)(2,1)S(1)}, u32[]{:S(2)}) copy-start(bf16[1,256,512]{2,1,0:T(8,128)(2,1)S(1)} %fusion.74) | copy-start | bytes 786436
  50.1 62.9 %copy-start.76 = (bf16[1,256,512]{2,1,0:T(8,128)(2,1)}, bf16[1,256,512]{2,1,0:T(8,128)(2,1)S(1)}, u32[]{:S(2)}) copy-start(bf16[1,256,512]{2,1,0:T(8,128)(2,1)S(1)} %fusion.75) | copy-start | bytes 786436
  51.0 290.7 %collective-permute-start.2 = (bf16[2,256,512]{2,1,0:T(8,128)(2,1)}, bf16[2,256,512]{2,1,0:T(8,128)(2,1)}, u32[]{:S(2)}, u32[]{:S(2)}) collective-permute-start(bf16[2,256,512]{2,1,0:T(8,128)(2,1)} %pad_maximum_fusion.13), channel_id=1, source_target_pairs={{4,0},{8,4},{12,8},{16,12},{20,16},{24,20},{28,24},{5,1},{9,5},{13... | collective-permute-start | bytes 1572872 | tf_op jit(solution)/shard_map/ppermute | solution.py:31
  52.3 289.4 %collective-permute-start.1 = (bf16[2,256,512]{2,1,0:T(8,128)(2,1)}, bf16[2,256,512]{2,1,0:T(8,128)(2,1)}, u32[]{:S(2)}, u32[]{:S(2)}) collective-permute-start(bf16[2,256,512]{2,1,0:T(8,128)(2,1)} %pad_maximum_fusion.13), channel_id=1, source_target_pairs={{0,4},{4,8},{8,12},{12,16},{16,20},{20,24},{24,28},{1,5},{5,9},{9,... | collective-permute-start | bytes 1572872 | tf_op jit(solution)/shard_map/ppermute | solution.py:29
  68.5 49.7 %copy-start.156 = (s32[256]{0:T(256)}, s32[256]{0:T(256)S(1)}, u32[]{:S(2)}) copy-start(s32[256]{0:T(256)S(1)} %get-tuple-element.954) | copy-start | bytes 3076
  114.2 235.8 %collective-permute-start.3 = (bf16[2,256,512]{2,1,0:T(8,128)(2,1)}, bf16[2,256,512]{2,1,0:T(8,128)(2,1)}, u32[]{:S(2)}, u32[]{:S(2)}) collective-permute-start(bf16[2,256,512]{2,1,0:T(8,128)(2,1)} %pad_maximum_fusion.14), channel_id=1, source_target_pairs={{0,4},{4,8},{8,12},{12,16},{16,20},{20,24},{24,28},{1,5},{5,9},{9,... | collective-permute-start | bytes 1572872 | tf_op jit(solution)/shard_map/ppermute | solution.py:18
  116.3 478.9 %reduce-scatter.71.cloned.1.call-start = ((), (), s32[]{:S(2)}) async-start(), calls=%async_computation.42 | async-start | bytes 655360
  119.6 195.9 %copy-start.78 = (bf16[256,512]{1,0:T(8,128)(2,1)}, bf16[256,512]{1,0:T(8,128)(2,1)S(1)}, u32[]{:S(2)}) copy-start(bf16[256,512]{1,0:T(8,128)(2,1)S(1)} %convolution_convert_fusion.34) | copy-start | bytes 786436
  119.6 50.0 %copy-start.177 = (bf16[128]{0:T(256)(128)(2,1)S(1)}, bf16[128]{0:T(256)(128)(2,1)}, u32[]{:S(2)}) copy-start(bf16[128]{0:T(256)(128)(2,1)} %param.118) | copy-start | bytes 772
  119.7 57.5 %copy-start.178 = (bf16[128]{0:T(256)(128)(2,1)S(1)}, bf16[128]{0:T(256)(128)(2,1)}, u32[]{:S(2)}) copy-start(bf16[128]{0:T(256)(128)(2,1)} %param.119) | copy-start | bytes 772
  119.7 67.0 %copy-start.179 = (bf16[128]{0:T(256)(128)(2,1)S(1)}, bf16[128]{0:T(256)(128)(2,1)}, u32[]{:S(2)}) copy-start(bf16[128]{0:T(256)(128)(2,1)} %param.120) | copy-start | bytes 772
  297.9 68.9 %copy-start.21 = (bf16[512,512]{1,0:T(8,128)(2,1)}, bf16[512,512]{1,0:T(8,128)(2,1)S(1)}, u32[]{:S(2)}) copy-start(bf16[512,512]{1,0:T(8,128)(2,1)S(1)} %all_gather.38) | copy-start | bytes 1572868
  313.7 53.7 %copy-start.23 = (bf16[512,512]{1,0:T(8,128)(2,1)}, bf16[512,512]{1,0:T(8,128)(2,1)S(1)}, u32[]{:S(2)}) copy-start(bf16[512,512]{1,0:T(8,128)(2,1)S(1)} %all_gather.43) | copy-start | bytes 1572868
  335.0 17.1 %collective-permute-start = (bf16[2,256,512]{2,1,0:T(8,128)(2,1)}, bf16[2,256,512]{2,1,0:T(8,128)(2,1)}, u32[]{:S(2)}, u32[]{:S(2)}) collective-permute-start(bf16[2,256,512]{2,1,0:T(8,128)(2,1)} %pad_maximum_fusion.10), channel_id=1, source_target_pairs={{0,4},{4,8},{8,12},{12,16},{16,20},{20,24},{24,28},{1,5},{5,9},{9,... | collective-permute-start | bytes 1572872 | tf_op jit(solution)/shard_map/ppermute | solution.py:18
  426.8 13.2 %collective-permute-start.8 = (bf16[2,256,512]{1,2,0:T(8,128)(2,1)S(1)}, bf16[2,256,512]{1,2,0:T(8,128)(2,1)S(1)}, u32[]{:S(2)}, u32[]{:S(2)}) collective-permute-start(bf16[2,256,512]{1,2,0:T(8,128)(2,1)S(1)} %get-tuple-element.870), channel_id=1, source_target_pairs={{0,4},{4,8},{8,12},{12,16},{16,20},{20,24},{24,28},{1,5},{5,9},{9,... | collective-permute-start | bytes 1572872 | tf_op jit(solution)/shard_map/ppermute | solution.py:29
  430.3 9.7 collective-permute-start.9
  444.3 152.7 %reduce-scatter.67.cloned.1.call-start = ((), (), s32[]{:S(2)}) async-start(), calls=%async_computation.40 | async-start | bytes 655360
  454.2 144.5 %reduce-scatter.73.cloned.1.call-start = ((), (), s32[]{:S(2)}) async-start(), calls=%async_computation.43 | async-start | bytes 655360
  456.5 9.2 collective-permute-start.10
  462.2 3.8 collective-permute-start.11
  470.2 130.1 %reduce-scatter.69.cloned.1.call-start = ((), (), s32[]{:S(2)}) async-start(), calls=%async_computation.41 | async-start | bytes 655360
  474.5 127.4 %reduce-scatter.57.cloned.1.call-start = ((), (), s32[]{:S(2)}) async-start(), calls=%async_computation.35 | async-start | bytes 655360 | tf_op jit(solution)/shard_map/reduce_scatter | solution.py:462
  476.8 125.1 %reduce-scatter.55.cloned.1.call-start = ((), (), s32[]{:S(2)}) async-start(), calls=%async_computation.34 | async-start | bytes 655360 | tf_op jit(solution)/shard_map/reduce_scatter | solution.py:462
  479.1 122.9 %reduce-scatter.51.cloned.1.call-start = ((), (), s32[]{:S(2)}) async-start(), calls=%async_computation.32 | async-start | bytes 655360 | tf_op jit(solution)/shard_map/reduce_scatter | solution.py:444
  483.5 138.2 %reduce-scatter.53.cloned.1.call-start = ((), (), s32[]{:S(2)}) async-start(), calls=%async_computation.33 | async-start | bytes 655360 | tf_op jit(solution)/shard_map/reduce_scatter | solution.py:444
  489.4 154.5 %reduce-scatter.49.cloned.1.call-start = ((), (), s32[]{:S(2)}) async-start(), calls=%async_computation.31 | async-start | bytes 655360 | tf_op jit(solution)/shard_map/reduce_scatter | solution.py:438
  494.6 171.4 %reduce-scatter.47.cloned.1.call-start = ((), (), s32[]{:S(2)}) async-start(), calls=%async_computation.30 | async-start | bytes 655360 | tf_op jit(solution)/shard_map/reduce_scatter | solution.py:438
  502.7 185.5 %reduce-scatter.35.cloned.1.call-start = ((), (), s32[]{:S(2)}) async-start(), calls=%async_computation.24 | async-start | bytes 655360 | tf_op jit(solution)/shard_map/reduce_scatter | solution.py:420
  514.1 12.7 %collective-permute-start.6 = (bf16[2,256,512]{1,2,0:T(8,128)(2,1)}, bf16[2,256,512]{1,2,0:T(8,128)(2,1)}, u32[]{:S(2)}, u32[]{:S(2)}) collective-permute-start(bf16[2,256,512]{1,2,0:T(8,128)(2,1)} %pad_maximum_fusion.19), channel_id=1, source_target_pairs={{4,0},{8,4},{12,8},{16,12},{20,16},{24,20},{28,24},{5,1},{9,5},{13... | collective-permute-start | bytes 1572872 | tf_op jit(solution)/shard_map/ppermute | solution.py:18
  517.4 193.0 %reduce-scatter.37.cloned.1.call-start = ((), (), s32[]{:S(2)}) async-start(), calls=%async_computation.25 | async-start | bytes 655360 | tf_op jit(solution)/shard_map/reduce_scatter | solution.py:420
  524.5 207.9 %reduce-scatter.39.cloned.1.call-start = ((), (), s32[]{:S(2)}) async-start(), calls=%async_computation.26 | async-start | bytes 655360 | tf_op jit(solution)/shard_map/reduce_scatter | solution.py:426
  530.0 224.4 %reduce-scatter.43.cloned.1.call-start = ((), (), s32[]{:S(2)}) async-start(), calls=%async_computation.28 | async-start | bytes 655360 | tf_op jit(solution)/shard_map/reduce_scatter | solution.py:432
  534.9 11.0 collective-permute-start.7
  537.4 239.7 %reduce-scatter.41.cloned.1.call-start = ((), (), s32[]{:S(2)}) async-start(), calls=%async_computation.27 | async-start | bytes 655360 | tf_op jit(solution)/shard_map/reduce_scatter | solution.py:426
  547.4 251.7 %reduce-scatter.45.cloned.1.call-start = ((), (), s32[]{:S(2)}) async-start(), calls=%async_computation.29 | async-start | bytes 655360 | tf_op jit(solution)/shard_map/reduce_scatter | solution.py:432
  548.6 295.0 %reduce-scatter.63.cloned.1.call-start = ((), (), s32[]{:S(2)}) async-start(), calls=%async_computation.38 | async-start | bytes 2621440 | tf_op jit(solution)/shard_map/reduce_scatter | solution.py:474
  552.9 336.1 %reduce-scatter.65.cloned.1.call-start = ((), (), s32[]{:S(2)}) async-start(), calls=%async_computation.39 | async-start | bytes 2621440 | tf_op jit(solution)/shard_map/reduce_scatter | solution.py:474
  558.1 376.4 %reduce-scatter.61.cloned.1.call-start = ((), (), s32[]{:S(2)}) async-start(), calls=%async_computation.37 | async-start | bytes 2621440 | tf_op jit(solution)/shard_map/reduce_scatter | solution.py:468
  562.6 417.6 %reduce-scatter.59.cloned.1.call-start = ((), (), s32[]{:S(2)}) async-start(), calls=%async_computation.36 | async-start | bytes 2621440 | tf_op jit(solution)/shard_map/reduce_scatter | solution.py:468
  565.0 436.5 %reduce-scatter.75.cloned.1.call-start = ((), (), s32[]{:S(2)}) async-start(), calls=%async_computation.44 | async-start | bytes 163840
  592.6 429.1 %reduce-scatter.77.cloned.1.call-start = ((), (), s32[]{:S(2)}) async-start(), calls=%async_computation.45 | async-start | bytes 163840
  593.8 521.0 %all-reduce.21.cloned.1.call-start = ((), (), s32[]{:S(2)}) async-start(), calls=%async_computation.46 | async-start | bytes 8388608 | tf_op jit(solution)/shard_map/psum | solution.py:419
  (179 other events, 1243.3 us)
Sparse Core Ops, SparseCore 0:
  49.6 63.4 all-gather.8
  116.5 51.9 all-gather.10
  444.4 22.3 reduce-scatter.70
  468.9 19.9 reduce-scatter.66
  491.0 19.8 reduce-scatter.72
  513.0 20.0 reduce-scatter.68
  535.4 19.9 reduce-scatter.56
  557.6 19.9 reduce-scatter.54
  579.8 19.5 reduce-scatter.50
  601.6 20.0 reduce-scatter.52
  624.0 19.9 reduce-scatter.48
  646.1 19.9 reduce-scatter.46
  668.3 19.9 reduce-scatter.34
  690.4 19.9 reduce-scatter.36
  712.5 19.8 reduce-scatter.38
  734.5 19.8 reduce-scatter.42
  757.2 19.8 reduce-scatter.40
  779.2 19.8 reduce-scatter.44
  801.4 42.1 reduce-scatter.62
  845.8 43.1 reduce-scatter.64
  891.3 43.1 reduce-scatter.60
  937.0 43.1 reduce-scatter.58
  983.0 18.4 reduce-scatter.74
  1004.2 17.4 reduce-scatter.76
  1028.6 86.1 all-reduce.20
where the time goes:
time: 1140 us; the launch traced here: 1130 us
  waiting for transfers between devices  493 us (43%)
  blocking collectives  250 us (22%)
  local copies, waits for them, and re-layouts  153 us (13%)
  matrix products  132 us (12%)
  other arithmetic  54.4 us (5%)
  starting transfers between devices  30.4 us (3%)
  between operations  18.1 us (2%)
    reduce_scatter x2, waiting for transfers between devices, on_device(): lax.psum_scatter(micro_grads[8].astype(jnp.bfloat16), 'fsdp', scatter_dim...  91.1 us
    reduce_scatter x2, waiting for transfers between devices, on_device(): lax.psum_scatter(micro_grads[9].astype(jnp.bfloat16), 'fsdp', scatter_dim...  89.9 us
    psum x1, waiting for transfers between devices, on_device(): lax.psum(lax.psum_scatter(micro_grads[0].astype(jnp.bfloat16), 'fsdp', sc...  65.5 us
    reduce_scatter x2, waiting for transfers between devices, on_device(): lax.psum_scatter(micro_grads[1].astype(jnp.bfloat16), 'fsdp', scatter_dim...  44.7 us
    reduce_scatter x2, waiting for transfers between devices, on_device(): lax.psum_scatter(micro_grads[3].astype(jnp.bfloat16), 'fsdp', scatter_dim...  44.4 us
    reduce_scatter x2, waiting for transfers between devices, on_device(): lax.psum_scatter(micro_grads[0].astype(jnp.bfloat16), 'fsdp', scatter_dim...  44.3 us
    reduce_scatter x2, waiting for transfers between devices, on_device(): lax.psum_scatter(micro_grads[2].astype(jnp.bfloat16), 'fsdp', scatter_dim...  44.1 us
    gather x24, local copies, waits for them, and re-layouts, on_device(): seg_starts = jnp.searchsorted(seg_full, seg_rows, side='left')  41.3 us
  transfers between devices with their start and end apart: 37, of which 19 were waited for; matrix products, arithmetic and copies ran while one was open for 24% of the time, Pallas kernels for 0%

commit v1 on v0

v1 whole, which is shorter than its diff:
```python
import functools

import jax
import jax.numpy as jnp
from jax import lax
from jax.experimental import pallas as pl
from jax.experimental.pallas import tpu as pltpu
from jax.sharding import PartitionSpec as P

HEADS = 8
HEAD_DIM = 64
MAXLEN = 256
LANES = 128
SMALL_ROWS = 32
TAG_ROW = 6
EPSILON = 1e-05
MASKED = -1e30
SCALE = HEAD_DIM ** (-0.5)
BF16 = jnp.bfloat16
F32 = jnp.float32
MIB = 2**20

NN = (((1,), (0,)), ((), ()))
NT = (((1,), (1,)), ((), ()))
TN = (((0,), (0,)), ((), ()))


def dot(left, right, dims=NN):
    return lax.dot_general(left, right, dims, preferred_element_type=F32)


def lane_ids(rows):
    return lax.broadcasted_iota(jnp.int32, (rows, LANES), 1)


def norm_rows(values_in):
    center = values_in - jnp.mean(values_in, -1, keepdims=True)
    inverse = lax.rsqrt(jnp.mean(center * center, -1, keepdims=True) + EPSILON)
    return center * inverse, inverse


def norm_back(grad_rows, unit_rows, inverse, gain):
    scaled = grad_rows * gain
    centered = (
        scaled
        - jnp.mean(scaled, -1, keepdims=True)
        - unit_rows * jnp.mean(scaled * unit_rows, -1, keepdims=True)
    )
    return inverse * centered


def column_sums(values_in):
    return jnp.sum(values_in, 0, keepdims=True)


def attend(queries, keys, values, query_hot, key_bias, own_bias, exps_ref):
    rows, width = queries.shape[0], keys.shape[0]
    low = lane_ids(rows) < HEAD_DIM
    ones = jnp.ones((width, LANES), BF16)
    mixes, inverses = [], []
    for pair in range(HEADS // 2):
        cols = slice(LANES * pair, LANES * (pair + 1))
        pair_q = queries[:, cols]
        pair_k = jnp.concatenate([keys[:, cols], key_bias], 1)
        pair_v = jnp.concatenate([values[:, cols], ones], 1)
        sums = []
        for half in (0, 1):
            mine = low if half == 0 else ~low
            head_q = jnp.concatenate([jnp.where(mine, pair_q, jnp.zeros_like(pair_q)), query_hot], 1)
            scores = dot(head_q, pair_k, NT)
            if own_bias is not None:
                near = width - rows
                scores = jnp.concatenate([scores[:, :near], scores[:, near:] + own_bias], 1)
            highest = jnp.max(scores, -1, keepdims=True)
            exps = jnp.exp(scores - highest).astype(BF16)
            exps_ref[0, 2 * pair + half] = exps
            sums.append(dot(exps, pair_v))
        inverse = 1.0 / jnp.where(low, sums[0][:, LANES:], sums[1][:, LANES:])
        mixes.append(jnp.where(low, sums[0][:, :LANES], sums[1][:, :LANES]) * inverse)
        inverses.append(inverse)
    return jnp.concatenate(mixes, 1), jnp.concatenate(inverses, 1)


def attend_back(queries, keys, values, exps_ref, mix, inverse, grad_mix):
    rows, width = queries.shape[0], keys.shape[0]
    lane = lane_ids(rows)
    low = lane < HEAD_DIM
    low_wide = lane_ids(width) < HEAD_DIM
    two_ones = jnp.where(lane_ids(width) < 2, 1.0, 0.0).astype(BF16)
    grads_q, grads_k, grads_v = [], [], []
    for pair in range(HEADS // 2):
        cols = slice(LANES * pair, LANES * (pair + 1))
        pair_q, pair_k = queries[:, cols], keys[:, cols]
        pair_v = jnp.concatenate([values[:, cols], two_ones], 1)
        scaled = (grad_mix[:, cols].astype(F32) * inverse[:, cols]).astype(BF16)
        product = scaled.astype(F32) * mix[:, cols]
        found_q, found_k, found_v = [], [], []
        for half in (0, 1):
            mine = low if half == 0 else ~low
            centre = jnp.sum(jnp.where(mine, product, 0.0), -1, keepdims=True)
            coarse = centre.astype(BF16).astype(F32)
            shift = jnp.where(lane == 0, -coarse, jnp.where(lane == 1, coarse - centre, 0.0))
            head_g = jnp.concatenate(
                [jnp.where(mine, scaled, jnp.zeros_like(scaled)), shift.astype(BF16)], 1
            )
            exps = exps_ref[0, 2 * pair + half]
            grad_scores = (exps.astype(F32) * dot(head_g, pair_v, NT)).astype(BF16)
            found_q.append(dot(grad_scores, pair_k))
            found_k.append(dot(grad_scores, pair_q, TN))
            found_v.append(dot(exps, scaled, TN))
        grads_q.append(jnp.where(low, found_q[0], found_q[1]) * SCALE)
        grads_k.append(jnp.where(low_wide, found_k[0], found_k[1]))
        grads_v.append(jnp.where(low_wide, found_v[0], found_v[1]))
    return [jnp.concatenate(part, 1).astype(BF16) for part in (grads_q, grads_k, grads_v)]


def matrix(ref, number, width=512):
    return ref[:, number * width : (number + 1) * width]


def self_forward(
    shards,
    before_ref,
    here_ref,
    hot_ref,
    tag_ref,
    bias_ref,
    own_ref,
    weight_ref,
    start_ref,
    low_ref,
    q_ref,
    k_ref,
    v_ref,
    mix_ref,
    inv_ref,
    exps_ref,
    small_ref,
):
    rows = here_ref.shape[1]
    block = 512 // shards
    smalls = jnp.concatenate(
        [
            weight_ref[z * block : z * block + SMALL_ROWS, 1536 : 1536 + block]
            for z in range(shards)
        ],
        1,
    )
    small_ref[...] = smalls.astype(F32)
    seg_tags = dot(tag_ref[0], smalls, TN).astype(BF16)
    hot = hot_ref[0, : MAXLEN + rows]
    tokens = jnp.concatenate([before_ref[0], here_ref[0]], 0).astype(F32)
    start = tokens + dot(hot, seg_tags)
    start_ref[0] = start[MAXLEN:]
    start_low = start.astype(BF16)
    low_ref[0] = start_low
    queries = (dot(start_low[MAXLEN:], matrix(weight_ref, 0)).astype(BF16).astype(F32) * SCALE).astype(BF16)
    keys = dot(start_low, matrix(weight_ref, 1)).astype(BF16)
    values = dot(start_low, matrix(weight_ref, 2)).astype(BF16)
    q_ref[0] = queries
    k_ref[0] = keys
    v_ref[0] = values
    mix_ref[0], inv_ref[0] = attend(
        queries, keys, values, hot[MAXLEN:], bias_ref[0], own_ref[0], exps_ref
    )


def cross_forward(
    start_ref,
    self_mix_ref,
    before_ref,
    here_ref,
    after_ref,
    hot_ref,
    bias_ref,
    small_ref,
    weight_ref,
    norm_low_ref,
    unit_one_ref,
    scale_one_ref,
    q_ref,
    k_ref,
    v_ref,
    mix_ref,
    inv_ref,
    exps_ref,
    normed_ref,
    unit_two_ref,
    scale_two_ref,
):
    rows = start_ref.shape[1]
    source = jnp.concatenate([before_ref[0], here_ref[0], after_ref[0]], 0)
    keys = dot(source, matrix(weight_ref, 2)).astype(BF16)
    values = dot(source, matrix(weight_ref, 3)).astype(BF16)
    k_ref[0] = keys
    v_ref[0] = values
    branch = dot(self_mix_ref[0].astype(BF16), matrix(weight_ref, 0))
    unit_one, scale_one = norm_rows(start_ref[0] + branch)
    unit_one_ref[0] = unit_one
    scale_one_ref[0] = jnp.broadcast_to(scale_one, (rows, LANES))
    normed_one = unit_one * small_ref[0:1] + small_ref[1:2]
    norm_low = normed_one.astype(BF16)
    norm_low_ref[0] = norm_low
    queries = (dot(norm_low, matrix(weight_ref, 1)).astype(BF16).astype(F32) * SCALE).astype(BF16)
    q_ref[0] = queries
    mix, inverse = attend(
        queries, keys, values, hot_ref[0, MAXLEN : MAXLEN + rows], bias_ref[0], None, exps_ref
    )
    mix_ref[0] = mix
    inv_ref[0] = inverse
    branch = dot(mix.astype(BF16), matrix(weight_ref, 4))
    unit_two, scale_two = norm_rows(normed_one + branch)
    unit_two_ref[0] = unit_two
    scale_two_ref[0] = jnp.broadcast_to(scale_two, (rows, LANES))
    normed_ref[0] = unit_two * small_ref[2:3] + small_ref[3:4]


GELU_A = 0.7978845608028654
GELU_B = 0.044715


def feed_both(
    normed_ref,
    unit_ref,
    scale_ref,
    cotangent_ref,
    small_ref,
    weight_ref,
    out_ref,
    back_ref,
    grad_ref,
    sums_ref,
    act_ref,
    slope_ref,
):
    normed = normed_ref[...]
    normed_low = normed.astype(BF16)
    chunks = weight_ref.shape[1] // 1024
    feed = normed
    for part in range(chunks):
        cols = slice(512 * part, 512 * (part + 1))
        hidden = dot(normed_low, matrix(weight_ref, part))
        square = hidden * hidden
        bend = jnp.tanh(hidden * (GELU_A + GELU_A * GELU_B * square))
        rise = 0.5 + 0.5 * bend
        act = (hidden * rise).astype(BF16)
        act_ref[:, cols] = act
        slope_ref[:, cols] = rise + rise * (1.0 - bend) * hidden * (
            GELU_A + 3.0 * GELU_A * GELU_B * square
        )
        feed = feed + dot(act, matrix(weight_ref, chunks + part))
    unit, scale = norm_rows(feed)
    gain = small_ref[4:5]
    out_ref[...] = (unit * gain + small_ref[5:6]).astype(BF16)
    grad = cotangent_ref[...].astype(F32)
    sums_ref[...] = jnp.zeros_like(sums_ref)
    sums_ref[4:5] = column_sums(grad * unit)
    sums_ref[5:6] = column_sums(grad)
    d_three = norm_back(grad, unit, scale, gain)
    d_feed = d_three.astype(BF16)
    total = d_three
    for part in range(chunks):
        cols = slice(512 * part, 512 * (part + 1))
        late = slice(512 * (chunks + part), 512 * (chunks + part + 1))
        grad_ref[:, late] = dot(act_ref[:, cols], d_feed, TN).astype(BF16)
        d_hidden = (
            slope_ref[:, cols] * dot(d_feed, matrix(weight_ref, chunks + part), NT)
        ).astype(BF16)
        grad_ref[:, cols] = dot(normed_low, d_hidden, TN).astype(BF16)
        total = total + dot(d_hidden, matrix(weight_ref, part), NT)
    unit_two = unit_ref[...]
    sums_ref[2:3] = column_sums(total * unit_two)
    sums_ref[3:4] = column_sums(total)
    back_ref[...] = norm_back(total, unit_two, scale_ref[:, 0:1], small_ref[2:3])


def cross_backward(
    back_ref,
    self_mix_ref,
    before_ref,
    here_ref,
    after_ref,
    norm_low_ref,
    unit_ref,
    scale_ref,
    q_ref,
    k_ref,
    v_ref,
    mix_ref,
    inv_ref,
    exps_ref,
    small_ref,
    weight_ref,
    one_ref,
    source_before_ref,
    source_here_ref,
    source_after_ref,
    grad_ref,
    sums_ref,
    total_ref,
):
    step = pl.program_id(0)
    rows = here_ref.shape[1]

    @pl.when(step == 0)
    def _():
        total_ref[...] = jnp.zeros_like(total_ref)
        sums_ref[...] = jnp.zeros_like(sums_ref)

    def add(number, value):
        cols = slice(512 * number, 512 * (number + 1))
        total_ref[:, cols] = total_ref[:, cols] + value

    d_two = back_ref[0]
    d_branch = d_two.astype(BF16)
    mix = mix_ref[0]
    add(4, dot(mix.astype(BF16), d_branch, TN))
    d_mix = dot(d_branch, matrix(weight_ref, 4), NT).astype(BF16)
    d_q, d_k, d_v = attend_back(q_ref[0], k_ref[0], v_ref[0], exps_ref, mix, inv_ref[0], d_mix)
    source = jnp.concatenate([before_ref[0], here_ref[0], after_ref[0]], 0)
    add(2, dot(source, d_k, TN))
    add(3, dot(source, d_v, TN))
    d_source = dot(d_k, matrix(weight_ref, 2), NT) + dot(d_v, matrix(weight_ref, 3), NT)
    source_before_ref[0] = d_source[:MAXLEN].astype(BF16)
    source_here_ref[0] = d_source[MAXLEN : MAXLEN + rows]
    source_after_ref[0] = d_source[MAXLEN + rows :].astype(BF16)
    add(1, dot(norm_low_ref[0], d_q, TN))
    total = d_two + dot(d_q, matrix(weight_ref, 1), NT)
    unit = unit_ref[0]
    sums_ref[0:1] = sums_ref[0:1] + column_sums(total * unit)
    sums_ref[1:2] = sums_ref[1:2] + column_sums(total)
    d_one = norm_back(total, unit, scale_ref[0, :, 0:1], small_ref[0:1])
    one_ref[0] = d_one
    add(0, dot(self_mix_ref[0].astype(BF16), d_one.astype(BF16), TN))

    @pl.when(step == pl.num_programs(0) - 1)
    def _():
        grad_ref[...] = total_ref[...].astype(BF16)


def self_backward(
    shards,
    one_ref,
    low_ref,
    hot_ref,
    tag_ref,
    q_ref,
    k_ref,
    v_ref,
    mix_ref,
    inv_ref,
    exps_ref,
    feed_sums_ref,
    cross_sums_ref,
    out_weight_ref,
    weight_ref,
    before_ref,
    here_ref,
    grad_ref,
    total_ref,
    sums_ref,
):
    step = pl.program_id(0)
    rows = one_ref.shape[1]

    @pl.when(step == 0)
    def _():
        total_ref[...] = jnp.zeros_like(total_ref)
        sums_ref[...] = feed_sums_ref[...] + cross_sums_ref[...]

    def add(number, value):
        cols = slice(512 * number, 512 * (number + 1))
        total_ref[:, cols] = total_ref[:, cols] + value

    d_one = one_ref[0]
    d_mix = dot(d_one.astype(BF16), out_weight_ref[...], NT).astype(BF16)
    d_q, d_k, d_v = attend_back(
        q_ref[0], k_ref[0], v_ref[0], exps_ref, mix_ref[0], inv_ref[0], d_mix
    )
    start_low = low_ref[0]
    add(0, dot(start_low[MAXLEN:], d_q, TN))
    add(1, dot(start_low, d_k, TN))
    add(2, dot(start_low, d_v, TN))
    d_start = dot(d_k, matrix(weight_ref, 1), NT) + dot(d_v, matrix(weight_ref, 2), NT)
    d_before = d_start[:MAXLEN].astype(BF16)
    d_here = d_start[MAXLEN:] + d_one + dot(d_q, matrix(weight_ref, 0), NT)
    before_ref[0] = d_before
    here_ref[0] = d_here
    both = jnp.concatenate([d_before, d_here.astype(BF16)], 0)
    seg_sums = dot(hot_ref[0, : MAXLEN + rows], both, TN)
    coarse = seg_sums.astype(BF16)
    fine = (seg_sums - coarse.astype(F32)).astype(BF16)
    sums_ref[...] = sums_ref[...] + dot(tag_ref[0], coarse) + dot(tag_ref[0], fine)

    @pl.when(step == pl.num_programs(0) - 1)
    def _():
        grad_ref[:, :1536] = total_ref[...].astype(BF16)
        grad_ref[:, 1536:] = jnp.zeros((512, LANES), BF16)
        block = 512 // shards
        for z in range(shards):
            grad_ref[z * block : z * block + SMALL_ROWS, 1536 : 1536 + block] = sums_ref[
                :, z * block : (z + 1) * block
            ].astype(BF16)


def per_step(array):
    rest = (0,) * (array.ndim - 1)
    return pl.BlockSpec((1,) + array.shape[1:], lambda step: (step,) + rest)


def whole(array):
    rest = (0,) * array.ndim
    return pl.BlockSpec(array.shape, lambda step: rest)


def run_steps(body, name, stepped, fixed, stepped_outs, fixed_outs, scratch=(), order=None):
    batch = stepped[0].shape[0]
    outs = [jax.ShapeDtypeStruct(*spec) for spec in (*stepped_outs, *fixed_outs)]
    count = len(stepped_outs)
    return pl.pallas_call(
        body,
        grid=(batch,),
        in_specs=[per_step(a) for a in stepped] + [whole(a) for a in fixed],
        out_specs=[per_step(a) for a in outs[:count]] + [whole(a) for a in outs[count:]],
        out_shape=outs,
        scratch_shapes=list(scratch),
        compiler_params=pltpu.CompilerParams(vmem_limit_bytes=48 * MIB),
        name=name,
    )(*stepped, *fixed)


def gather_weights(*packs):
    return [lax.all_gather(pack, "fsdp", axis=0, tiled=True) for pack in packs]


def reduce_grads(*grads):
    return [
        lax.psum(lax.psum_scatter(grad, "fsdp", scatter_dimension=0, tiled=True), "seq")
        for grad in grads
    ]


def local_facts(seg_ids, keep_mask, pair_tags, cut_lo, cut_hi, base, rows):
    sentences = pair_tags.shape[1]
    ids = jnp.arange(sentences, dtype=jnp.int32)
    starts = jnp.sum(seg_ids[:, :, None] < ids, 1, dtype=jnp.int32)
    ends = jnp.sum(seg_ids[:, :, None] <= ids, 1, dtype=jnp.int32)
    half = (ends - starts - 1) // 2
    spare = ((0, 0), (0, LANES - sentences))
    lower = jnp.pad(starts + jnp.minimum(cut_lo, half), spare)
    upper = jnp.pad(ends - jnp.minimum(cut_hi, half), spare)
    edge = ((0, 0), (MAXLEN, MAXLEN))
    width = rows + 2 * MAXLEN
    seg = lax.dynamic_slice_in_dim(jnp.pad(seg_ids, edge, constant_values=-1), base, width, 1)
    keep = lax.dynamic_slice_in_dim(jnp.pad(keep_mask, edge), base, width, 1)
    lanes = jnp.arange(LANES, dtype=jnp.int32)
    hot = seg[:, :, None] == lanes
    place = base - MAXLEN + jnp.arange(width, dtype=jnp.int32)[None, :, None]
    inside = (place >= lower[:, None, :]) & (place < upper[:, None, :])
    near = MAXLEN + rows
    seen = (keep[:, :near] == 1) | (jnp.arange(near) >= MAXLEN)
    self_bias = jnp.where(hot[:, :near] & seen[:, :, None], 0.0, MASKED).astype(BF16)
    cross_bias = jnp.where(inside, 0.0, MASKED).astype(BF16)
    spot = jnp.arange(rows, dtype=jnp.int32)
    earlier = (spot[None, :] < spot[:, None]) & (keep[:, None, MAXLEN:near] == 1)
    own_bias = jnp.where(earlier | (spot[None, :] == spot[:, None]), 0.0, MASKED).astype(F32)
    tag_rows = TAG_ROW + pair_tags
    tags = (tag_rows[:, None, :] == jnp.arange(SMALL_ROWS, dtype=jnp.int32)[:, None]).astype(BF16)
    tags = jnp.pad(tags, ((0, 0), (0, 0), (0, LANES - sentences)))
    return hot.astype(BF16), self_bias, cross_bias, own_bias, tags


def shifted(shard, by):
    size = lax.axis_size("seq")
    pairs = [(i, i + by) for i in range(size) if 0 <= i + by < size]
    return lax.ppermute(shard, "seq", pairs)


def on_device(
    inputs,
    encoded,
    cotangent,
    seg_ids,
    keep_mask,
    pair_tags,
    cut_lo,
    cut_hi,
    w_query,
    w_key,
    w_value,
    w_out,
    c_query,
    c_key,
    c_value,
    c_out,
    w_up,
    w_down,
    gain_one,
    bias_one,
    gain_two,
    bias_two,
    gain_three,
    bias_three,
    tag_table,
):
    batch, rows, _ = inputs.shape
    shards = lax.axis_size("fsdp")
    block = w_query.shape[0]
    chunks = w_down.shape[0] // block
    base = lax.axis_index("seq") * rows
    small = jnp.concatenate(
        [
            jnp.stack([gain_one, bias_one, gain_two, bias_two, gain_three, bias_three]),
            tag_table,
        ],
        0,
    )
    small = jnp.pad(small, ((0, block - small.shape[0]), (0, LANES - small.shape[1])))
    up = w_up.reshape(block, shards, chunks, block).swapaxes(1, 2).reshape(block, -1)
    down = w_down.reshape(chunks, block, 512).swapaxes(0, 1).reshape(block, -1)
    pack_one = jnp.concatenate([w_query, w_key, w_value, small], 1)
    pack_two = jnp.concatenate([w_out, c_query, c_key, c_value, c_out], 1)
    pack_three = jnp.concatenate([up, down], 1)
    full_one, full_two, full_three = gather_weights(pack_one, pack_two, pack_three)

    inputs_before = shifted(inputs, 1)
    encoded_before = shifted(encoded, 1)
    encoded_after = shifted(encoded, -1)
    hot, self_bias, cross_bias, own_bias, tags = local_facts(
        seg_ids, keep_mask, pair_tags, cut_lo, cut_hi, base, rows
    )
    near, wide = MAXLEN + rows, 2 * MAXLEN + rows

    def tokens(count, kind, width=512):
        return ((batch, count, width), kind)

    start, start_low, s_q, s_k, s_v, s_mix, s_inv, s_exps, smalls = run_steps(
        functools.partial(self_forward, shards),
        "self_forward",
        (inputs_before, inputs, hot, tags, self_bias, own_bias),
        (full_one,),
        (
            tokens(rows, F32),
            tokens(near, BF16),
            tokens(rows, BF16),
            tokens(near, BF16),
            tokens(near, BF16),
            tokens(rows, F32),
            tokens(rows, F32),
            ((batch, HEADS, rows, near), BF16),
        ),
        (((SMALL_ROWS, 512), F32),),
    )
    (
        norm_low,
        unit_one,
        scale_one,
        c_q,
        c_k,
        c_v,
        c_mix,
        c_inv,
        c_exps,
        normed_two,
        unit_two,
        scale_two,
    ) = run_steps(
        cross_forward,
        "cross_forward",
        (start, s_mix, encoded_before, encoded, encoded_after, hot, cross_bias),
        (smalls, full_two),
        (
            tokens(rows, BF16),
            tokens(rows, F32),
            tokens(rows, F32, LANES),
            tokens(rows, BF16),
            tokens(wide, BF16),
            tokens(wide, BF16),
            tokens(rows, F32),
            tokens(rows, F32),
            ((batch, HEADS, rows, wide), BF16),
            tokens(rows, F32),
            tokens(rows, F32),
            tokens(rows, F32, LANES),
        ),
        (),
    )
    count = batch * rows
    hidden = 512 * chunks

    def flat(array):
        return array.reshape(count, array.shape[-1])

    output, d_two, grad_three, feed_sums = pl.pallas_call(
        feed_both,
        out_shape=[
            jax.ShapeDtypeStruct((count, 512), BF16),
            jax.ShapeDtypeStruct((count, 512), F32),
            jax.ShapeDtypeStruct((512, 2 * hidden), BF16),
            jax.ShapeDtypeStruct((SMALL_ROWS, 512), F32),
        ],
        scratch_shapes=[pltpu.VMEM((count, hidden), BF16), pltpu.VMEM((count, hidden), F32)],
        compiler_params=pltpu.CompilerParams(vmem_limit_bytes=48 * MIB),
        name="feed_both",
    )(flat(normed_two), flat(unit_two), flat(scale_two), flat(cotangent), smalls, full_three)
    d_one, source_before, source_here, source_after, grad_two, cross_sums = run_steps(
        cross_backward,
        "cross_backward",
        (
            d_two.reshape(batch, rows, 512),
            s_mix,
            encoded_before,
            encoded,
            encoded_after,
            norm_low,
            unit_one,
            scale_one,
            c_q,
            c_k,
            c_v,
            c_mix,
            c_inv,
            c_exps,
        ),
        (smalls, full_two),
        (
            tokens(rows, F32),
            tokens(MAXLEN, BF16),
            tokens(rows, F32),
            tokens(MAXLEN, BF16),
        ),
        (((512, 2560), BF16), ((SMALL_ROWS, 512), F32)),
        (pltpu.VMEM((512, 2560), F32),),
    )
    grad_encoded = (source_here + shifted(source_before, -1) + shifted(source_after, 1)).astype(BF16)
    start_before, start_here, grad_one = run_steps(
        functools.partial(self_backward, shards),
        "self_backward",
        (d_one, start_low, hot, tags, s_q, s_k, s_v, s_mix, s_inv, s_exps),
        (feed_sums, cross_sums, full_two[:, :512], full_one),
        (tokens(MAXLEN, BF16), tokens(rows, F32)),
        (((512, 1536 + LANES), BF16),),
        (pltpu.VMEM((512, 1536), F32), pltpu.VMEM((SMALL_ROWS, 512), F32)),
    )
    grad_inputs = (start_here + shifted(start_before, -1)).astype(BF16)
    grad_one, grad_two, grad_three = reduce_grads(grad_one, grad_two, grad_three)

    def part(array, number):
        return array[:, 512 * number : 512 * (number + 1)].astype(F32)

    small_sums = grad_one[:, 1536:].astype(F32)
    grad_up = grad_three[:, :hidden].reshape(block, chunks, shards, block).swapaxes(1, 2)
    grad_down = grad_three[:, hidden:].reshape(block, chunks, 512).swapaxes(0, 1)
    return (
        output.reshape(batch, rows, 512),
        grad_inputs,
        grad_encoded,
        part(grad_one, 0),
        part(grad_one, 1),
        part(grad_one, 2),
        part(grad_two, 0),
        part(grad_two, 1),
        part(grad_two, 2),
        part(grad_two, 3),
        part(grad_two, 4),
        grad_up.reshape(block, hidden).astype(F32),
        grad_down.reshape(chunks * block, 512).astype(F32),
        *(small_sums[row, :block] for row in range(TAG_ROW)),
        small_sums[TAG_ROW : TAG_ROW + tag_table.shape[0], :block],
    )


def solution(mesh):
    rows = P("fsdp", "seq", None)
    by_row = P("fsdp", None)
    vector = P("fsdp")
    tags = P(None, "fsdp")
    return jax.shard_map(
        on_device,
        mesh=mesh,
        in_specs=(rows,) * 3 + (by_row,) * 15 + (vector,) * 6 + (tags,),
        out_specs=(rows,) * 3 + (by_row,) * 10 + (vector,) * 6 + (tags,),
        check_vma=False,
    )
```

time: 1140 us -> 502 us (0.44)
  blocking collectives: 250 us -> 0 us
  waiting for transfers between devices: 493 us -> 360 us
  matrix products: 132 us -> 0 us
  local copies, waits for them, and re-layouts: 153 us -> 28.4 us
  Pallas kernels: 0 us -> 70 us
  other arithmetic: 54.4 us -> 12.2 us
  starting transfers between devices: 30.4 us -> 15.9 us
    reduce_scatter x16 -> x3, waiting for transfers between devices: 378 us -> 165 us  [reduce_grads(): lax.psum_scatter(grad, 'fsdp', scatter_dimension=0, tiled=True)]
    all_gather x15 -> x0, blocking collectives: 209 us -> none  [the longest x1 21.6 us: fetch_weights(): lax.all_gather(w_value, 'fsdp', axis=0, tiled=True)]
    dot_general x88 -> x0, matrix products: 132 us -> none  [the longest x20 36.8 us: dot_first(): lax.dot_general(left, right, (((0,), (0,)), ((), ())), preferred_element_...]
    all_gather x2 -> x3, waiting for transfers between devices: 0.02 us -> 131 us  [gather_weights(): return [lax.all_gather(pack, 'fsdp', axis=0, tiled=True) for pack in packs]]
    gather x48 -> x0, local copies, waits for them, and re-layouts: 82.7 us -> none  [the longest x24 41.3 us: on_device(): seg_starts = jnp.searchsorted(seg_full, seg_rows, side='left')]
    pallas_call x0 -> x5, Pallas kernels: none -> 70 us  [the longest x4 57.4 us: run_steps(): pl.pallas_call(body, grid=(batch,), in_specs=[per_step(a) for a in steppe...]
    unnamed x31 -> x7, waiting for transfers between devices: 38.1 us -> 1.14 us
    psum x1 -> x0, blocking collectives: 23.1 us -> none  [on_device(): lax.psum(lax.psum_scatter(micro_grads[10].astype(jnp.bfloat16), 'fsdp', s...]
  transfers between devices with their start and end apart: 37 -> 13, of which waited for: 19 -> 7; matrix products, arithmetic and copies ran while one was open for 24% -> 2% of each run, Pallas kernels for 0% -> 4%
where the time goes in v1:
time: 502 us; the launch traced here: 501 us
  waiting for transfers between devices  360 us (72%)
  Pallas kernels  70 us (14%)
  local copies, waits for them, and re-layouts  28.4 us (6%)
  starting transfers between devices  15.9 us (3%)
  between operations  14.7 us (3%)
  other arithmetic  12.2 us (2%)
    reduce_scatter x3, waiting for transfers between devices, reduce_grads(): lax.psum_scatter(grad, 'fsdp', scatter_dimension=0, tiled=True)  165 us
    all_gather x3, waiting for transfers between devices, gather_weights(): return [lax.all_gather(pack, 'fsdp', axis=0, tiled=True) for pack in packs]  131 us
    psum x1, waiting for transfers between devices, reduce_grads(): lax.psum(lax.psum_scatter(grad, 'fsdp', scatter_dimension=0, tiled=True),...  62.8 us
    pallas_call x4, Pallas kernels, run_steps(): pl.pallas_call(body, grid=(batch,), in_specs=[per_step(a) for a in steppe...  57.4 us
    unnamed x79, local copies, waits for them, and re-layouts  18.8 us
    ppermute x6, starting transfers between devices, shifted(): return lax.ppermute(shard, 'seq', pairs)  15.7 us
    pallas_call x1, Pallas kernels, on_device(): pl.pallas_call(feed_both, out_shape=[jax.ShapeDtypeStruct((count, 512), B...  12.7 us
  transfers between devices with their start and end apart: 13, of which 7 were waited for; matrix products, arithmetic and copies ran while one was open for 2% of the time, Pallas kernels for 4%

profile of v1, /device:TPU:0, one launch (start us, length us, event | category | flops | bytes accessed | tf_op | source)
XLA Modules:
  0.0 501.2 jit_solution(12524783122454794472)
XLA Ops:
  7.3 1.6 concatenate.12
  8.9 1.8 fusion.1
  10.8 0.9 constant_dynamic-update-slice_fusion.4
  11.7 0.9 constant_dynamic-update-slice_fusion.3
  12.6 0.9 constant_dynamic-update-slice_fusion.2
  13.6 0.8 copy-done.26
  16.1 1.1 pad_maximum_fusion
  17.3 2.4 collective-permute-start.1
  19.7 1.3 collective-permute-start.2
  21.0 5.9 %collective-permute-start = (bf16[2,256,512]{2,1,0:T(8,128)(2,1)}, bf16[2,256,512]{2,1,0:T(8,128)(2,1)}, u32[]{:S(2)}, u32[]{:S(2)}) collective-permute-start(bf16[2,256,512]{2,1,0:T(8,128)(2,1)} %here_ref.3), channel_id=1, source_target_pairs={{0,4},{4,8},{8,12},{12,16},{16,20},{20,24},{24,28},{1,5},{5,9},{9,... | collective-permute-start | bytes 1572872 | tf_op jit(solution)/shard_map/ppermute | solution.py:476
  28.2 24.7 %all-gather.4.cloned.1.call-done.weight_ref = bf16[512,1664]{1,0:T(8,128)(2,1)} async-done(((bf16[128,1664]{1,0:T(8,128)(2,1)}), bf16[512,1664]{1,0:T(8,128)(2,1)}) %all-gather.4.cloned.1.call-update) | async-done | bytes 1703952 | tf_op jit(solution)/shard_map/all_gather | solution.py:433
  52.9 8.5 %self_forward.1 = (f32[2,256,512]{2,1,0:T(8,128)S(1)}, bf16[2,512,512]{2,1,0:T(8,128)(2,1)S(1)}, bf16[2,256,512]{2,1,0:T(8,128)(2,1)S(1)}, bf16[2,512,512]{2,1,0...) custom-call(bf16[2,256,512]{2,1,0:T(8,128)(2,1)} %collective-permute, ...), custom_call_target="tpu_custom_call" | custom-call | tf_op jit(solution)/shard_map/self_forward/pallas_call | solution.py:420
  61.3 1.0 copy-done.1
  62.4 1.0 copy-done.7
  63.4 1.0 copy-done.9
  64.4 0.8 copy-done.17
  65.2 42.9 %all-gather.6.cloned.1.call-done.weight_ref = bf16[512,2560]{1,0:T(8,128)(2,1)} async-done(((bf16[128,2560]{1,0:T(8,128)(2,1)}), bf16[512,2560]{1,0:T(8,128)(2,1)}) %all-gather.6.cloned.1.call-update) | async-done | bytes 2621456 | tf_op jit(solution)/shard_map/all_gather | solution.py:433
  108.1 1.1 slice.89.out_weight_ref
  109.2 12.7 %cross_forward.1 = (bf16[2,256,512]{2,1,0:T(8,128)(2,1)S(1)}, f32[2,256,512]{2,1,0:T(8,128)S(1)}, f32[2,256,128]{2,1,0:T(8,128)S(1)}, bf16[2,256,512]{2,1,0:T(8,...) custom-call(f32[2,256,512]{2,1,0:T(8,128)} %copy-done.1, ...), custom_call_target="tpu_custom_call" | custom-call | tf_op jit(solution)/shard_map/cross_forward/pallas_call | solution.py:420
  121.9 1.0 copy-done.2
  122.9 1.0 copy-done.3
  123.9 0.8 copy-done.13
  124.7 0.8 copy-done.15
  126.1 63.1 %all-gather.8.cloned.1.call-done.weight_ref = bf16[512,4096]{1,0:T(8,128)(2,1)} async-done(((bf16[128,4096]{1,0:T(8,128)(2,1)}), bf16[512,4096]{1,0:T(8,128)(2,1)}) %all-gather.8.cloned.1.call-update) | async-done | bytes 4194320 | tf_op jit(solution)/shard_map/all_gather | solution.py:433
  189.3 1.2 copy-done.5
  190.5 1.2 copy-done.6
  191.7 1.0 copy-done.12
  192.8 12.7 %feed_both.1 = (bf16[512,512]{1,0:T(8,128)(2,1)}, f32[512,512]{1,0:T(8,128)S(1)}, bf16[512,4096]{1,0:T(8,128)(2,1)}, f32[32,512]{1,0:T(8,128)S(1)}) custom-call(f32[512,512]{1,0:T(8,128)S(1)} %bitcast.35, f32[512,512]{1,0:T(8,128)S(1)} %bitcast.36, f32[512,128]{1,0:T(8,128)S(1)} %bitcast.38, bf16[512,512]{1,0:T(8,128)(2,1)S(1)} %bitcast.37, ...), custom_call_target="tpu_custom_call" | custom-call | tf_op jit(solution)/shard_map/feed_both/pallas_call | solution.py:594
  205.4 1.0 copy-done.4
  206.4 0.8 copy-done.11
  207.2 20.3 %cross_backward.1 = (f32[2,256,512]{2,1,0:T(8,128)S(1)}, bf16[2,256,512]{2,1,0:T(8,128)(2,1)S(1)}, f32[2,256,512]{2,1,0:T(8,128)S(1)}, bf16[2,256,512]{2,1,0:T(8...) custom-call(f32[2,256,512]{2,1,0:T(8,128)} %bitcast.34, ...), custom_call_target="tpu_custom_call" | custom-call | tf_op jit(solution)/shard_map/cross_backward/pallas_call | solution.py:420
  227.6 0.8 copy-done.23
  228.4 15.9 %self_backward.1 = (bf16[2,256,512]{2,1,0:T(8,128)(2,1)S(1)}, f32[2,256,512]{2,1,0:T(8,128)S(1)}, bf16[512,1664]{1,0:T(8,128)(2,1)}) custom-call(f32[2,256,512]{2,1,0:T(8,128)S(1)} %get-tuple-element.71.one_ref, bf16[2,512,512]{2,1,0:T(8,128)(2,1)S(1)} %copy-done.8, bf16[2,768,128]{2,1,0:T(8,128)(2,1)S(1)} %get-tuple-element.112.hot_ref, ...), custom_call_target="tpu_custom_call" | custom-call | tf_op jit(solution)/shard_map/self_backward/pallas_call | solution.py:420
  244.3 0.8 copy-done.25
  246.3 1.4 collective-permute-start.3
  247.8 33.4 %reduce-scatter.4.cloned.1.call-done = bf16[128,1664]{1,0:T(8,128)(2,1)} async-done(((bf16[512,1664]{1,0:T(8,128)(2,1)}), bf16[128,1664]{1,0:T(8,128)(2,1)}) %reduce-scatter.4.cloned.1.call-update) | async-done | bytes 426000 | tf_op jit(solution)/shard_map/reduce_scatter | solution.py:438
  281.1 53.3 %reduce-scatter.6.cloned.1.call-done = bf16[128,2560]{1,0:T(8,128)(2,1)} async-done(((bf16[512,2560]{1,0:T(8,128)(2,1)}), bf16[128,2560]{1,0:T(8,128)(2,1)}) %reduce-scatter.6.cloned.1.call-update) | async-done | bytes 655376 | tf_op jit(solution)/shard_map/reduce_scatter | solution.py:438
  334.5 78.6 %reduce-scatter.8.cloned.1.call-done = bf16[128,4096]{1,0:T(8,128)(2,1)} async-done(((bf16[512,4096]{1,0:T(8,128)(2,1)}), bf16[128,4096]{1,0:T(8,128)(2,1)}) %reduce-scatter.8.cloned.1.call-update) | async-done | bytes 1048592 | tf_op jit(solution)/shard_map/reduce_scatter | solution.py:438
  413.1 1.6 collective-permute-start.4
  414.7 3.1 collective-permute-start.5
  417.8 2.0 add_convert_fusion.1
  419.8 1.0 add_convert_fusion
  420.8 62.8 %all-reduce.9.cloned.1.call-done = (bf16[128,1664]{1,0:T(8,128)(2,1)}, bf16[128,2560]{1,0:T(8,128)(2,1)}, bf16[128,4096]{1,0:T(8,128)(2,1)}) async-done(((bf16[128,1664]{1,0:T(8,128)(2,1)}, bf16[128,2560]{1,0:T(8,128)(2,1)}, bf16[128,4096]{1,0:T(8,128)(2,1)}), (bf16[128,1664]{1,0:T(8,128)(2,1)}, bf16[128,2560]{1,0:T(8,128)(2,1)}, bf16[128,4096]{1,0:T(8,128)(2,1)})) %all-reduce.9.cloned.1.call-update) | async-done | bytes 2129936 | tf_op jit(solution)/shard_map/psum | solution.py:438
  483.6 1.9 slice_convert_fusion.7
  487.4 1.4 slice_convert_fusion
  489.8 1.4 reshape.133
  491.9 1.3 copy.52
  493.2 1.1 slice_convert_fusion.2
  (109 shorter events, 8.4 us)
Async XLA Ops:
  7.2 6.4 %copy-start.30 = (bf16[128,512]{1,0:T(8,128)(2,1)S(1)}, bf16[128,512]{1,0:T(8,128)(2,1)}, u32[]{:S(2)}) copy-start(bf16[128,512]{1,0:T(8,128)(2,1)} %param.39) | copy-start | bytes 393220
  7.2 6.4 %copy-start.31 = (bf16[128,512]{1,0:T(8,128)(2,1)S(1)}, bf16[128,512]{1,0:T(8,128)(2,1)}, u32[]{:S(2)}) copy-start(bf16[128,512]{1,0:T(8,128)(2,1)} %param.40) | copy-start | bytes 393220
  7.2 7.3 %copy-start.28 = (bf16[128,2048]{1,0:T(8,128)(2,1)S(1)}, bf16[128,2048]{1,0:T(8,128)(2,1)}, u32[]{:S(2)}) copy-start(bf16[128,2048]{1,0:T(8,128)(2,1)} %param.41) | copy-start | bytes 1572868
  7.2 45.6 %all-gather.4.cloned.1.call-start = ((), (), s32[]{:S(2)}) async-start(), calls=%async_computation.3 | async-start | bytes 2129920 | tf_op jit(solution)/shard_map/all_gather | solution.py:433
  10.8 97.4 %all-gather.6.cloned.1.call-start = ((), (), s32[]{:S(2)}) async-start(), calls=%async_computation.4 | async-start | bytes 3276800 | tf_op jit(solution)/shard_map/all_gather | solution.py:433
  13.6 1.9 copy-start.29
  13.6 0.8 copy-start.26
  14.5 174.8 %all-gather.8.cloned.1.call-start = ((), (), s32[]{:S(2)}) async-start(), calls=%async_computation.5 | async-start | bytes 5242880 | tf_op jit(solution)/shard_map/all_gather | solution.py:433
  15.9 1.3 copy-start
  16.0 11.0 %copy-start.32 = (s32[2,2048]{1,0:T(2,128)S(1)}, s32[2,2048]{1,0:T(2,128)}, u32[]{:S(2)}) copy-start(s32[2,2048]{1,0:T(2,128)} %param.28) | copy-start | bytes 49156
  16.0 11.0 %copy-start.35 = (s32[2,16]{1,0:T(2,128)S(1)}, s32[2,16]{1,0:T(2,128)}, u32[]{:S(2)}) copy-start(s32[2,16]{1,0:T(2,128)} %param.30) | copy-start | bytes 388
  16.0 11.3 %copy-start.33 = (s32[2,2048]{1,0:T(2,128)S(1)}, s32[2,2048]{1,0:T(2,128)}, u32[]{:S(2)}) copy-start(s32[2,2048]{1,0:T(2,128)} %param.29) | copy-start | bytes 49156
  16.0 11.3 %copy-start.34 = (s32[2,16]{1,0:T(2,128)S(1)}, s32[2,16]{1,0:T(2,128)}, u32[]{:S(2)}) copy-start(s32[2,16]{1,0:T(2,128)} %param.31) | copy-start | bytes 388
  16.0 11.3 %copy-start.36 = (s32[2,16]{1,0:T(2,128)S(1)}, s32[2,16]{1,0:T(2,128)}, u32[]{:S(2)}) copy-start(s32[2,16]{1,0:T(2,128)} %param.32) | copy-start | bytes 388
  17.2 263.9 %reduce-scatter.4.cloned.1.call-start = ((), (), s32[]{:S(2)}) async-start(), calls=%async_computation.6 | async-start | bytes 2129920 | tf_op jit(solution)/shard_map/reduce_scatter | solution.py:438
  17.3 91.9 %collective-permute-start.1 = (bf16[2,256,512]{2,1,0:T(8,128)(2,1)S(1)}, bf16[2,256,512]{2,1,0:T(8,128)(2,1)S(1)}, u32[]{:S(2)}, u32[]{:S(2)}) collective-permute-start(bf16[2,256,512]{2,1,0:T(8,128)(2,1)S(1)} %copy-done), channel_id=1, source_target_pairs={{0,4},{4,8},{8,12},{12,16},{16,20},{20,24},{24,28},{1,5},{5,9},{9,... | collective-permute-start | bytes 1572872 | tf_op jit(solution)/shard_map/ppermute | solution.py:476
  19.7 89.5 %collective-permute-start.2 = (bf16[2,256,512]{2,1,0:T(8,128)(2,1)S(1)}, bf16[2,256,512]{2,1,0:T(8,128)(2,1)S(1)}, u32[]{:S(2)}, u32[]{:S(2)}) collective-permute-start(bf16[2,256,512]{2,1,0:T(8,128)(2,1)S(1)} %copy-done), channel_id=1, source_target_pairs={{4,0},{8,4},{12,8},{16,12},{20,16},{24,20},{28,24},{5,1},{9,5},{13... | collective-permute-start | bytes 1572872 | tf_op jit(solution)/shard_map/ppermute | solution.py:476
  21.0 7.2 %collective-permute-start = (bf16[2,256,512]{2,1,0:T(8,128)(2,1)}, bf16[2,256,512]{2,1,0:T(8,128)(2,1)}, u32[]{:S(2)}, u32[]{:S(2)}) collective-permute-start(bf16[2,256,512]{2,1,0:T(8,128)(2,1)} %here_ref.3), channel_id=1, source_target_pairs={{0,4},{4,8},{8,12},{12,16},{16,20},{20,24},{24,28},{1,5},{5,9},{9,... | collective-permute-start | bytes 1572872 | tf_op jit(solution)/shard_map/ppermute | solution.py:476
  61.3 1.0 copy-start.1
  62.4 1.0 copy-start.7
  63.4 1.0 copy-start.9
  64.4 0.8 copy-start.17
  65.2 124.1 %copy-start.10 = (f32[32,512]{1,0:T(8,128)}, f32[32,512]{1,0:T(8,128)S(1)}, u32[]{:S(2)}) copy-start(f32[32,512]{1,0:T(8,128)S(1)} %get-tuple-element.56.small_ref) | copy-start | bytes 196612
  121.9 1.0 copy-start.2
  122.9 1.0 copy-start.3
  123.9 0.8 copy-start.13
  124.7 0.8 copy-start.15
  189.3 1.2 copy-start.5
  190.5 1.2 copy-start.6
  191.7 1.0 copy-start.12
  192.7 13.6 %copy-start.14 = (bf16[2,256,512]{2,1,0:T(8,128)(2,1)S(1)}, bf16[2,256,512]{2,1,0:T(8,128)(2,1)}, u32[]{:S(2)}) copy-start(bf16[2,256,512]{2,1,0:T(8,128)(2,1)} %copy-done.13) | copy-start | bytes 1572868
  192.7 13.7 %copy-start.16 = (bf16[2,256,512]{2,1,0:T(8,128)(2,1)S(1)}, bf16[2,256,512]{2,1,0:T(8,128)(2,1)}, u32[]{:S(2)}) copy-start(bf16[2,256,512]{2,1,0:T(8,128)(2,1)} %copy-done.15) | copy-start | bytes 1572868
  192.8 13.7 %copy-start.20 = (f32[2,256,128]{2,1,0:T(8,128)S(1)}, f32[2,256,128]{2,1,0:T(8,128)}, u32[]{:S(2)}) copy-start(f32[2,256,128]{2,1,0:T(8,128)} %copy-done.19) | copy-start | bytes 786436
  205.4 1.0 copy-start.4
  206.4 0.8 copy-start.11
  207.2 21.1 %copy-start.8 = (bf16[2,512,512]{2,1,0:T(8,128)(2,1)S(1)}, bf16[2,512,512]{2,1,0:T(8,128)(2,1)}, u32[]{:S(2)}) copy-start(bf16[2,512,512]{2,1,0:T(8,128)(2,1)} %copy-done.7) | copy-start | bytes 3145732
  207.2 21.1 %copy-start.18 = (bf16[2,256,512]{2,1,0:T(8,128)(2,1)S(1)}, bf16[2,256,512]{2,1,0:T(8,128)(2,1)}, u32[]{:S(2)}) copy-start(bf16[2,256,512]{2,1,0:T(8,128)(2,1)} %copy-done.17) | copy-start | bytes 1572868
  228.4 15.9 %copy-start.21 = (bf16[2,256,512]{2,1,0:T(8,128)(2,1)}, bf16[2,256,512]{2,1,0:T(8,128)(2,1)S(1)}, u32[]{:S(2)}) copy-start(bf16[2,256,512]{2,1,0:T(8,128)(2,1)S(1)} %get-tuple-element.84) | copy-start | bytes 1572868
  244.3 0.8 copy-start.25
  245.1 89.4 %reduce-scatter.6.cloned.1.call-start = ((), (), s32[]{:S(2)}) async-start(), calls=%async_computation.7 | async-start | bytes 3276800 | tf_op jit(solution)/shard_map/reduce_scatter | solution.py:438
  245.7 167.4 %reduce-scatter.8.cloned.1.call-start = ((), (), s32[]{:S(2)}) async-start(), calls=%async_computation.8 | async-start | bytes 5242880 | tf_op jit(solution)/shard_map/reduce_scatter | solution.py:438
  246.3 166.9 %copy-start.24 = (bf16[2,256,512]{2,1,0:T(8,128)(2,1)S(1)}, bf16[2,256,512]{2,1,0:T(8,128)(2,1)}, u32[]{:S(2)}) copy-start(bf16[2,256,512]{2,1,0:T(8,128)(2,1)} %copy-done.23) | copy-start | bytes 1572868
  246.3 168.4 %copy-start.22 = (bf16[2,256,512]{2,1,0:T(8,128)(2,1)S(1)}, bf16[2,256,512]{2,1,0:T(8,128)(2,1)}, u32[]{:S(2)}) copy-start(bf16[2,256,512]{2,1,0:T(8,128)(2,1)} %copy-done.21) | copy-start | bytes 1572868
  246.3 237.3 %all-reduce.9.cloned.1.call-start = ((), (), s32[]{:S(2)}) async-start(), calls=%async_computation.9 | async-start | bytes 4259840 | tf_op jit(solution)/shard_map/psum | solution.py:438
  246.3 171.5 %collective-permute-start.3 = (bf16[2,256,512]{2,1,0:T(8,128)(2,1)}, bf16[2,256,512]{2,1,0:T(8,128)(2,1)}, u32[]{:S(2)}, u32[]{:S(2)}) collective-permute-start(bf16[2,256,512]{2,1,0:T(8,128)(2,1)} %copy-done.25), channel_id=1, source_target_pairs={{4,0},{8,4},{12,8},{16,12},{20,16},{24,20},{28,24},{5,1},{9,5},{13... | collective-permute-start | bytes 1572872 | tf_op jit(solution)/shard_map/ppermute | solution.py:476
  413.1 6.7 %collective-permute-start.4 = (bf16[2,256,512]{2,1,0:T(8,128)(2,1)S(1)}, bf16[2,256,512]{2,1,0:T(8,128)(2,1)S(1)}, u32[]{:S(2)}, u32[]{:S(2)}) collective-permute-start(bf16[2,256,512]{2,1,0:T(8,128)(2,1)S(1)} %copy-done.24), channel_id=1, source_target_pairs={{4,0},{8,4},{12,8},{16,12},{20,16},{24,20},{28,24},{5,1},{9,5},{13... | collective-permute-start | bytes 1572872 | tf_op jit(solution)/shard_map/ppermute | solution.py:476
  414.7 5.1 %collective-permute-start.5 = (bf16[2,256,512]{2,1,0:T(8,128)(2,1)S(1)}, bf16[2,256,512]{2,1,0:T(8,128)(2,1)S(1)}, u32[]{:S(2)}, u32[]{:S(2)}) collective-permute-start(bf16[2,256,512]{2,1,0:T(8,128)(2,1)S(1)} %copy-done.22), channel_id=1, source_target_pairs={{0,4},{4,8},{8,12},{12,16},{16,20},{20,24},{24,28},{1,5},{5,9},{9,... | collective-permute-start | bytes 1572872 | tf_op jit(solution)/shard_map/ppermute | solution.py:476
  491.2 2.0 copy-start.27
  (2 other events, 1.5 us)
Sparse Core Ops, SparseCore 0:
  10.9 41.9 all-gather.3
  54.4 53.6 all-gather.5
  109.7 79.5 all-gather.7
  245.2 35.8 reduce-scatter.3
  283.3 51.1 reduce-scatter.5
  336.6 76.4 reduce-scatter.7
  417.1 66.4 all-reduce.8
